TPU v7x, 512 devices: a whole 4x8x8 slice. The times are simulated.
512 devices in a mesh: pb: 16 (over y, core), ka: 32 (over z, x).
Axes of the slice: x: 4, y: 8, z: 8, core: 2. Of those that a mesh axis runs over, the one named last changes fastest.
Arguments:
- coupling: bfloat16 [400, 2, 196608], P('pb', None, 'ka'), may hold values from -0.3125 to 0.3125
- eigvecs: bfloat16 [32, 8192], P('ka'), may hold values from -0.75 to 0.75
- partner: int32 [16, 32], P('pb', 'ka'), may hold values from 0 to 31
- kpoints: float32 [3, 32], replicated, may hold values from 0 to 1
- qpoints: float32 [3, 16], replicated, may hold values from 0 to 1
- lattice: int32 [6, 400], replicated, may hold values from -4 to 4
Outputs:
- couplings_sq: bfloat16 [16, 32, 196608], P('pb', 'ka')
All inputs are finite; a program needn't handle non-finite values.
Results may differ from a plain program's by a relative error of at most 0.008.
Values may be sent and summed in bfloat16 or wider, within the bound.
A program may use at most 64 MiB of HBM per device.

v0:
```python
import math

import jax
import jax.numpy as jnp
from jax import lax
from jax.sharding import PartitionSpec as P


def phase_pair(kpoints, qvector, lattice):
    lattice_f = lattice.astype(jnp.float32)
    kdot = (
        kpoints[0][:, None] * lattice_f[0][None, :]
        + kpoints[1][:, None] * lattice_f[1][None, :]
        + kpoints[2][:, None] * lattice_f[2][None, :]
    )
    qdot = (
        qvector[0][:, None] * lattice_f[3][None, :]
        + qvector[1][:, None] * lattice_f[4][None, :]
        + qvector[2][:, None] * lattice_f[5][None, :]
    )
    angle = 2.0 * math.pi * (kdot[None, :, :] + qdot[:, None, :])
    return (jnp.cos(angle).astype(jnp.bfloat16), jnp.sin(angle).astype(jnp.bfloat16))


def transform(cosines, sines, coupling):
    rows = coupling.shape[0]
    flat = coupling.reshape(rows, -1)
    count = cosines.shape[0]
    stacked = jnp.concatenate([cosines, sines], axis=0)
    both = jnp.dot(stacked, flat, preferred_element_type=jnp.float32).reshape(2 * count, 2, -1)
    with_cos = both[:count]
    with_sin = both[count:]
    real_part = with_cos[:, 0] - with_sin[:, 1]
    imag_part = with_cos[:, 1] + with_sin[:, 0]
    return jnp.stack([real_part, imag_part], axis=1).astype(jnp.bfloat16)


def rotate(bloch, far_vectors, near_vectors):
    count = bloch.shape[0]
    width = far_vectors.shape[1] // 2
    width = int(round_free(width))
    modes = bloch.shape[2] // (width * width)
    field = bloch.reshape(count, 2, width, width * modes)
    left = far_vectors.reshape(count, 2, width, width)
    right = near_vectors.reshape(count, 2, width, width)
    half_real = jnp.einsum(
        "kim,kix->kmx", left[:, 0], field[:, 0], preferred_element_type=jnp.float32
    ) + jnp.einsum("kim,kix->kmx", left[:, 1], field[:, 1], preferred_element_type=jnp.float32)
    half_imag = jnp.einsum(
        "kim,kix->kmx", left[:, 0], field[:, 1], preferred_element_type=jnp.float32
    ) - jnp.einsum("kim,kix->kmx", left[:, 1], field[:, 0], preferred_element_type=jnp.float32)
    half_real = half_real.astype(jnp.bfloat16).reshape(count, width, width, modes)
    half_imag = half_imag.astype(jnp.bfloat16).reshape(count, width, width, modes)
    joined = jnp.concatenate([half_real, half_imag], axis=2)
    joined = jnp.transpose(joined, (0, 1, 3, 2)).reshape(count, width * modes, 2 * width)
    top_rows = jnp.concatenate([right[:, 0], right[:, 1]], axis=2)
    low_rows = jnp.concatenate([-right[:, 1], right[:, 0]], axis=2)
    block = jnp.concatenate([top_rows, low_rows], axis=1)
    rotated = jnp.einsum("kxa,kab->kxb", joined, block, preferred_element_type=jnp.float32)
    squares = (
        rotated[:, :, :width] * rotated[:, :, :width]
        + rotated[:, :, width:] * rotated[:, :, width:]
    )
    squares = squares.astype(jnp.bfloat16).reshape(count, width, modes, width)
    return jnp.transpose(squares, (0, 1, 3, 2)).reshape(count, width * width * modes)


def round_free(value):
    return value**0.5


def body(coupling, eigvecs, partner, kpoints, qpoints, lattice):
    kpoint_count = eigvecs.shape[0]
    all_rows = lax.all_gather(coupling, "pb", axis=0, tiled=True)
    qvector = lax.dynamic_slice_in_dim(qpoints, lax.axis_index("pb"), 1, 1)
    cosines, sines = phase_pair(kpoints, qvector, lattice)
    bloch = transform(cosines[0], sines[0], all_rows)
    local_bloch = lax.all_to_all(bloch, "ka", split_axis=0, concat_axis=2, tiled=True)
    wanted = partner.reshape(-1)
    piece = lax.all_gather(eigvecs, "ka", axis=0, tiled=True)
    labels = jnp.arange(piece.shape[0], dtype=jnp.int32)
    select = (wanted[:, None] == labels[None, :]).astype(jnp.bfloat16)
    far_vectors = jnp.dot(select, piece, preferred_element_type=jnp.float32).astype(jnp.bfloat16)
    result = rotate(local_bloch, far_vectors, eigvecs)
    return result.reshape(1, kpoint_count, result.shape[1])


def solution(mesh):
    in_specs = (P("pb", None, "ka"), P("ka", None), P("pb", "ka"), P(), P(), P())
    out_specs = P("pb", "ka", None)
    return jax.shard_map(body, mesh=mesh, in_specs=in_specs, out_specs=out_specs, check_vma=False)
```

profile of v0, /device:TPU:2, one launch (start us, length us, event | category | flops | bytes accessed | tf_op | source)
XLA Modules:
  0.0 201.2 jit_solution(4325266138834154427)
XLA Ops:
  6.5 0.0 copy-start
  6.5 0.0 all-gather.3.cloned.1.call-start
  6.5 0.7 all-gather.3.cloned.1.call-update
  7.3 0.7 convert_element_type.33
  8.0 0.0 copy-done
  8.0 0.1 constant_dynamic-slice_fusion
  8.1 0.6 fusion.32
  8.7 0.8 slice_bitcast_fusion.16
  9.4 2.0 fusion.31
  11.4 0.3 cosine_convert_fusion
  11.7 67.4 %all-gather.3.cloned.1.call-done = bf16[400,2,6144]{2,1,0:T(2,128)(2,1)} async-done(((bf16[25,2,6144]{2,1,0:T(2,128)(2,1)}), bf16[400,2,6144]{2,1,0:T(2,128)(2,1)}) %all-gather.3.cloned.1.call-update) | async-done | bytes 9830416 | tf_op jit(solution)/shard_map/all_gather | solution.py:74
  79.2 11.8 %copy.19 = bf16[50,8,2,6144]{3,1,2,0:T(8,128)(2,1)} copy(bf16[50,8,2,6144]{3,2,1,0:T(2,128)(2,1)} %bitcast.68) | data formatting | bytes 19660800
  91.0 5.7 %fusion.11 = f32[64,12288]{1,0:T(8,128)S(1)} fusion(bf16[400,12288]{1,0:T(8,128)(2,1)} %bitcast.67, bf16[32,400]{1,0:T(8,128)(2,1)S(1)} %get-tuple-element.16, bf16[32,400]{1,0:T(8,128)(2,1)S(1)} %get-tuple-element.15), kind=kOutput, calls=%fused_computation.22 | convolution fusion | flops 629248000 | bytes 13027328 | tf_op jit(solution)/shard_map/dot_general | solution.py:30
  96.7 1.4 fusion.30
  98.1 2.7 %slice.118 = f32[32,2,6144]{2,1,0:T(2,128)S(1)} reshape(f32[32,12288]{1,0:T(8,128)} %get-tuple-element.8) | data formatting | bytes 3145728 | tf_op jit(solution)/shard_map/slice | solution.py:32
  100.8 2.5 %slice.115 = f32[32,2,6144]{2,1,0:T(2,128)} reshape(f32[32,12288]{1,0:T(8,128)S(1)} %get-tuple-element.7) | data formatting | bytes 3145728 | tf_op jit(solution)/shard_map/slice | solution.py:31
  103.2 4.3 %fusion.5 = (bf16[32,1,6144]{2,1,0:T(2,128)(2,1)S(1)}, bf16[32,1,6144]{2,1,0:T(2,128)(2,1)S(1)}) fusion(f32[32,2,6144]{2,1,0:T(2,128)S(1)} %slice.118, f32[32,2,6144]{2,1,0:T(2,128)} %slice.115), kind=kLoop, calls=%fused_computation.12 | loop fusion | flops 786432 | bytes 3932160 | tf_op jit(solution)/shard_map/convert
  107.5 0.0 copy-start.1
  107.6 2.7 %pad_maximum_fusion = bf16[32,2,6144]{2,1,0:T(2,128)(2,1)} fusion(bf16[32,1,6144]{2,1,0:T(2,128)(2,1)S(1)} %get-tuple-element.6, bf16[32,1,6144]{2,1,0:T(2,128)(2,1)S(1)} %get-tuple-element.5), kind=kLoop, calls=%fused_computation.13 | loop fusion | flops 1572864 | bytes 1572864 | tf_op jit(solution)/shard_map/stack | solution.py:35
  110.2 10.5 %all-to-all-start = ((bf16[32,2,6144]{2,1,0:T(2,128)(2,1)}), bf16[32,2,6144]{2,1,0:T(2,128)(2,1)S(1)}, u32[]{:S(2)}, u32[]{:S(2)}) async-start(bf16[32,2,6144]{2,1,0:T(2,128)(2,1)} %pad_maximum_fusion), calls=%async_computation | async-start | bytes 1572864 | tf_op jit(solution)/shard_map/all_to_all | solution.py:78
  121.4 0.0 copy-done.1
  121.4 61.6 %all-gather = bf16[32,1,8192]{2,1,0:T(2,128)(2,1)S(1)} all-gather(bf16[1,1,8192]{2,1,0:T(2,128)(2,1)S(1)} %bitcast.72), channel_id=1, replica_groups=mesh['pb'=16,'ka'=32] {'ka'}, dimensions={0}, use_global_device_ids=true | all-gather | bytes 540672 | tf_op jit(solution)/shard_map/all_gather | solution.py:80
  183.0 0.7 fusion.6
  183.7 0.1 reshape.223
  183.8 0.1 reduce
  183.9 0.1 reshape.233
  184.0 0.0 all-to-all-done
  184.0 0.2 copy.14
  184.2 0.3 reshape.226
  184.5 0.3 fusion.10
  184.8 0.3 fusion.9
  185.1 0.3 fusion.1
  185.4 1.1 reshape.231
  186.5 0.8 copy.16
  187.3 0.3 fusion
  187.6 1.1 reshape.230
  188.7 0.6 copy.15
  189.3 0.4 pad_maximum_fusion.1
  189.7 0.5 convolution_bitcast_fusion
  190.2 0.1 fusion.3
  190.3 1.1 reshape.235
  191.4 0.7 copy.17
  192.1 2.3 %reshape_reshape.3 = bf16[1,1,196608]{2,1,0:T(2,128)(2,1)} reshape(bf16[1,64,64,48]{3,2,1,0:T(8,128)(2,1)S(1)} %copy.17) | data formatting | bytes 786432 | tf_op jit(solution)/shard_map/reshape;reshape | solution.py:85
  (3 shorter events, 0.0 us)
Async XLA Ops:
  6.5 1.5 copy-start
  6.5 72.6 %all-gather.3.cloned.1.call-start = ((), (), s32[]{:S(2)}) async-start(), calls=%async_computation.1 | async-start | bytes 10444800 | tf_op jit(solution)/shard_map/all_gather | solution.py:74
  107.5 13.8 %copy-start.1 = (bf16[1,8192]{1,0:T(2,128)(2,1)S(1)}, bf16[1,8192]{1,0:T(2,128)(2,1)}, u32[]{:S(2)}) copy-start(bf16[1,8192]{1,0:T(2,128)(2,1)} %param.7) | copy-start | bytes 49156
  110.2 73.8 %all-to-all-start = ((bf16[32,2,6144]{2,1,0:T(2,128)(2,1)}), bf16[32,2,6144]{2,1,0:T(2,128)(2,1)S(1)}, u32[]{:S(2)}, u32[]{:S(2)}) async-start(bf16[32,2,6144]{2,1,0:T(2,128)(2,1)} %pad_maximum_fusion), calls=%async_computation | async-start | bytes 1572864 | tf_op jit(solution)/shard_map/all_to_all | solution.py:78
Sparse Core Ops, SparseCore 0:
  9.5 69.6 all-gather.2
where the time goes:
time: 202 us; the launch traced here: 201 us
  waiting for transfers between devices  68.1 us (34%)
  blocking collectives  61.6 us (30%)
  local copies, waits for them, and re-layouts  28.1 us (14%)
  between operations  14.2 us (7%)
  other arithmetic  10.6 us (5%)
  starting transfers between devices  10.5 us (5%)
  matrix products  7.98 us (4%)
    all_gather x1, waiting for transfers between devices, body(): all_rows = lax.all_gather(coupling, 'pb', axis=0, tiled=True)  67.4 us
    all_gather x1, blocking collectives, body(): piece = lax.all_gather(eigvecs, 'ka', axis=0, tiled=True)  61.6 us
    unnamed x5, local copies, waits for them, and re-layouts  11.8 us
    all_to_all x1, starting transfers between devices, body(): lax.all_to_all(bloch, 'ka', split_axis=0, concat_axis=2, tiled=True)  10.5 us
    dot_general x1, matrix products, transform(): jnp.dot(stacked, flat, preferred_element_type=jnp.float32)  5.72 us
    another operation x1, other arithmetic  4.3 us
  transfers between devices with their start and end apart: 2, of which 1 were waited for; matrix products, arithmetic and copies ran while one was open for 3% of the time, Pallas kernels for 0%

commit v1 on v0

v1 whole, which is shorter than its diff:
```python
import math

import jax
import jax.numpy as jnp
from jax import lax
from jax.experimental import pallas as pl
from jax.experimental.pallas import tpu as pltpu
from jax.sharding import PartitionSpec as P

MESH = pl.DeviceIdType.MESH
NPB = 16
NKA = 32
NZ = 8
NX = 4
VS = 3
F32 = jnp.float32
BF16 = jnp.bfloat16


def kernel(
    c_hbm, near_ref, eig_ref, part_ref, kp_ref, qp_ref, lat_ref, out_ref,
    ck, sk, cq, sq, phase, wmat, cols, bsend, brecv, table, parts, tmat, qsend, qrecv, spread,
    c_ss, c_rs, b_ss, b_rs, q_ss, q_rs, z_ss, z_rs, x_ss, x_rs, p_ss, p_rs, own_sem,
):
    pb = lax.axis_index("pb")
    ka = lax.axis_index("ka")
    zi = ka // NX
    xi = lax.rem(ka, NX)

    def pb_peer(step):
        return lax.rem(pb + step, NPB)

    def ka_peer(step):
        return lax.rem(ka + step, NKA)

    barrier = pltpu.get_barrier_semaphore()

    def greet_pb(step, carry):
        pl.semaphore_signal(barrier, inc=1, device_id=(pb_peer(step), ka), device_id_type=MESH)
        return carry

    def greet_ka(step, carry):
        pl.semaphore_signal(barrier, inc=1, device_id=(pb, ka_peer(step)), device_id_type=MESH)
        return carry

    lax.fori_loop(1, NPB, greet_pb, 0)
    lax.fori_loop(1, NKA, greet_ka, 0)

    own = pltpu.make_async_copy(c_hbm.at[pb], cols.at[:, pb], own_sem)
    own.start()

    def turn(points, first, extra):
        t = extra
        for axis in range(3):
            t = t + points[:, axis : axis + 1] * lat_ref[first + axis : first + axis + 1, :]
        return (2.0 * math.pi) * (t - jnp.round(t))

    ang = turn(kp_ref[...], 0, jnp.zeros((NKA, 1024), F32))
    ck[...] = jnp.cos(ang)
    sk[...] = jnp.sin(ang)
    ang = turn(qp_ref[...], 3, jnp.broadcast_to(lat_ref[6:7, :], (NPB, 1024)))
    cq[...] = jnp.cos(ang)
    sq[...] = jnp.sin(ang)

    wmat[...] = jnp.zeros_like(wmat)
    for i2 in range(2):
        rows0 = pl.ds(i2 * 64, 64)
        rows1 = pl.ds(128 + i2 * 64, 64)
        lanes0 = pl.ds(i2 * 128, 128)
        lanes1 = pl.ds(256 + i2 * 128, 128)
        wmat[rows0, lanes0] = near_ref[0]
        wmat[rows1, lanes0] = near_ref[1]
        wmat[rows0, lanes1] = -near_ref[1]
        wmat[rows1, lanes1] = near_ref[0]

    pl.semaphore_wait(barrier, NPB - 1 + NKA - 1)

    def c_copy(v, step):
        to = pb_peer(step)
        return pltpu.make_async_remote_copy(
            src_ref=c_hbm.at[to, v], dst_ref=cols.at[v, pb],
            send_sem=c_ss.at[v, to], recv_sem=c_rs.at[v, pb],
            device_id=(to, ka), device_id_type=MESH,
        )

    def c_recv(v, step):
        src = pb_peer(step)
        return pltpu.make_async_remote_copy(
            src_ref=c_hbm.at[src, v], dst_ref=cols.at[v, src],
            send_sem=c_ss.at[v, src], recv_sem=c_rs.at[v, src],
            device_id=(src, ka), device_id_type=MESH,
        )

    def z_copy(step, sending):
        other = lax.rem(zi + step, NZ)
        slot = zi if sending else other
        return pltpu.make_async_remote_copy(
            src_ref=eig_ref, dst_ref=table.at[xi, slot],
            send_sem=z_ss.at[other], recv_sem=z_rs.at[slot],
            device_id=(pb, other * NX + xi), device_id_type=MESH,
        )

    def x_copy(step, sending):
        other = lax.rem(xi + step, NX)
        slot = xi if sending else other
        return pltpu.make_async_remote_copy(
            src_ref=table.at[slot], dst_ref=table.at[slot],
            send_sem=x_ss.at[other], recv_sem=x_rs.at[slot],
            device_id=(pb, zi * NX + other), device_id_type=MESH,
        )

    def p_copy(step, sending):
        other = pb_peer(step)
        slot = pb if sending else other
        return pltpu.make_async_remote_copy(
            src_ref=part_ref, dst_ref=parts.at[slot],
            send_sem=p_ss.at[other], recv_sem=p_rs.at[slot],
            device_id=(other, ka), device_id_type=MESH,
        )

    def b_copy(v, step, sending):
        other = ka_peer(step)
        slot = ka if sending else other
        return pltpu.make_async_remote_copy(
            src_ref=bsend.at[v, other], dst_ref=brecv.at[v, slot],
            send_sem=b_ss.at[v, other], recv_sem=b_rs.at[v, slot],
            device_id=(pb, other), device_id_type=MESH,
        )

    def q_copy(v, step, sending):
        other = pb_peer(step)
        slot = pb if sending else other
        return pltpu.make_async_remote_copy(
            src_ref=qsend.at[v, other], dst_ref=qrecv.at[v, slot],
            send_sem=q_ss.at[v, other], recv_sem=q_rs.at[v, slot],
            device_id=(other, ka), device_id_type=MESH,
        )

    def loop(first, last, do):
        def step_of(step, carry):
            do(step)
            return carry

        lax.fori_loop(first, last, step_of, 0)

    loop(1, NPB, lambda s: c_copy(0, s).start())
    loop(1, NZ, lambda s: z_copy(s, True).start())
    loop(1, NPB, lambda s: c_copy(1, s).start())
    loop(1, NPB, lambda s: c_copy(2, s).start())
    loop(1, NPB, lambda s: p_copy(s, True).start())

    table[xi, zi] = eig_ref[...]
    parts[pb] = part_ref[...]

    def make_phase(k):
        c = ck[pl.ds(k, 1), :]
        s = sk[pl.ds(k, 1), :]
        phase[k, 0:16, :] = (c * cq[...] - s * sq[...]).astype(BF16)
        phase[k, 16:32, :] = (s * cq[...] + c * sq[...]).astype(BF16)

    loop(0, NKA, make_phase)

    loop(1, NZ, lambda s: z_copy(s, False).wait_recv())
    loop(1, NX, lambda s: x_copy(s, True).start())

    own.wait()

    def bloch_of(v):
        loop(1, NPB, lambda s: c_recv(v, s).wait_recv())

        def part(n):
            rows = pl.ds(n * 8, 8)
            got = jnp.dot(
                phase[rows].reshape(256, 1024), cols[v].reshape(1024, 128),
                preferred_element_type=F32,
            )
            bsend[v, rows] = got.astype(BF16).reshape(8, 32, 128)

        loop(0, 4, part)
        loop(1, NKA, lambda s: b_copy(v, s, True).start())
        brecv[v, ka] = bsend[v, ka]

    loop(0, VS, bloch_of)

    loop(1, NX, lambda s: x_copy(s, False).wait_recv())
    loop(1, NPB, lambda s: p_copy(s, False).wait_recv())

    low = lax.broadcasted_iota(jnp.int32, (32, 128), 1) < 64

    def squares(q):
        field = jnp.concatenate([tmat[t, pl.ds(q, 32, stride=16), :] for t in range(4)], axis=0)
        label = jnp.max(parts[q])
        far = table[lax.rem(label, NX), label // NX]
        turned = field.T.astype(BF16)
        got = lax.dot_general(
            turned, jnp.concatenate([far, far], axis=0), (((1,), (1,)), ((), ())),
            preferred_element_type=F32,
        )
        got = got * got
        both = got[0:64] + got[64:128]
        return jnp.where(low, both[0:32], both[32:64]).astype(BF16)

    def rotate(v):
        loop(1, NKA, lambda s: b_copy(v, s, False).wait_recv())

        def near(n):
            rows = pl.ds(n * 8, 8)
            field = jnp.concatenate(
                [brecv[v, rows, 0:16, :].reshape(128, 128), brecv[v, rows, 16:32, :].reshape(128, 128)],
                axis=1,
            )
            got = jnp.dot(field, wmat[...], preferred_element_type=F32)
            for t in range(4):
                tmat[t, pl.ds(n * 128, 128), :] = got[:, t * 128 : (t + 1) * 128]

        loop(0, 4, near)

        def one(s):
            q = pb_peer(s)
            qsend[v, q] = squares(q)
            q_copy(v, s, True).start()

        loop(1, NPB, one)
        qrecv[v, pb] = squares(pb)

    loop(0, VS, rotate)

    def place(v):
        loop(1, NPB, lambda s: q_copy(v, s, False).wait_recv())

        def one(s):
            spread[pl.ds(3 * s + v, 32, stride=48), :] = qrecv[v, s].astype(F32)

        loop(0, NPB, one)

    loop(0, VS, place)

    for n in range(12):
        block = spread[n * 128 : (n + 1) * 128, :].T.astype(BF16)
        out_ref[:, n * 128 : (n + 1) * 128] = block[0:64]
        out_ref[:, 1536 + n * 128 : 1536 + (n + 1) * 128] = block[64:128]

    loop(1, NZ, lambda s: z_copy(s, True).wait_send())
    loop(1, NX, lambda s: x_copy(s, True).wait_send())
    loop(1, NPB, lambda s: p_copy(s, True).wait_send())

    def drain(v):
        loop(1, NPB, lambda s: c_copy(v, s).wait_send())
        loop(1, NKA, lambda s: b_copy(v, s, True).wait_send())
        loop(1, NPB, lambda s: q_copy(v, s, True).wait_send())

    loop(0, VS, drain)


def couple(columns, near, eig, part, kp, qp, lat):
    vmem = pl.BlockSpec(memory_space=pltpu.VMEM)
    dma = pltpu.SemaphoreType.DMA
    return pl.pallas_call(
        kernel,
        out_shape=jax.ShapeDtypeStruct((64, 3072), BF16),
        in_specs=[pl.BlockSpec(memory_space=pl.ANY)] + [vmem] * 6,
        out_specs=vmem,
        scratch_shapes=[
            pltpu.VMEM((NKA, 1024), F32),
            pltpu.VMEM((NKA, 1024), F32),
            pltpu.VMEM((NPB, 1024), F32),
            pltpu.VMEM((NPB, 1024), F32),
            pltpu.VMEM((NKA, 32, 1024), BF16),
            pltpu.VMEM((256, 512), BF16),
            pltpu.VMEM((VS, NPB, 64, 128), BF16),
            pltpu.VMEM((VS, NKA, 32, 128), BF16),
            pltpu.VMEM((VS, NKA, 32, 128), BF16),
            pltpu.VMEM((NX, NZ, 64, 128), BF16),
            pltpu.VMEM((NPB, 8, 128), jnp.int32),
            pltpu.VMEM((4, 512, 128), F32),
            pltpu.VMEM((VS, NPB, 32, 128), BF16),
            pltpu.VMEM((VS, NPB, 32, 128), BF16),
            pltpu.VMEM((1536, 128), F32),
            dma((VS, NPB)), dma((VS, NPB)),
            dma((VS, NKA)), dma((VS, NKA)),
            dma((VS, NPB)), dma((VS, NPB)),
            dma((NZ,)), dma((NZ,)),
            dma((NX,)), dma((NX,)),
            dma((NPB,)), dma((NPB,)),
            dma(()),
        ],
        compiler_params=pltpu.CompilerParams(
            collective_id=0, has_side_effects=True, vmem_limit_bytes=40 << 20
        ),
        name="couple",
    )(columns, near, eig, part, kp, qp, lat)


def body(coupling, eigvecs, partner, kpoints, qpoints, lattice):
    columns = coupling.reshape(25, 2, 128, 48).transpose(3, 1, 0, 2)
    columns = jnp.pad(columns, ((0, 0), (0, 0), (0, 7), (0, 0))).reshape(NPB, VS, 64, 128)
    vectors = eigvecs.reshape(2, 64, 64)
    real, imag = vectors[0], vectors[1]
    near = jnp.stack([jnp.concatenate([real, imag], 1), jnp.concatenate([-imag, real], 1)])
    eig = vectors.reshape(2, 32, 2, 64).transpose(3, 0, 2, 1).reshape(64, 128)
    part = jnp.broadcast_to(partner, (8, 128))
    lat = jnp.pad(lattice.astype(F32).reshape(6, NPB, 1, 25), ((0, 0), (0, 0), (0, 0), (0, 7)))
    lat = jnp.broadcast_to(lat, (6, NPB, 2, 32)).reshape(6, 1024)
    quarter = jnp.broadcast_to(jnp.array([0.0, 0.25], F32).reshape(1, 1, 2, 1), (1, NPB, 2, 32))
    lat = jnp.concatenate([lat, quarter.reshape(1, 1024), jnp.zeros((1, 1024), F32)], 0)
    out = couple(columns, near, eig, part, kpoints.T, qpoints.T, lat)
    return out.reshape(1, 1, 196608)


def solution(mesh):
    in_specs = (P("pb", None, "ka"), P("ka", None), P("pb", "ka"), P(), P(), P())
    out_specs = P("pb", "ka", None)
    return jax.shard_map(body, mesh=mesh, in_specs=in_specs, out_specs=out_specs, check_vma=False)
```

time: 202 us -> 75.3 us (0.37)
  the two profiles are of different devices: /device:TPU:2 before, /device:TPU:1 now
where the time goes in v1:
time: 75.3 us; the launch traced here: 75.2 us
  Pallas kernels  67.3 us (89%)
  local copies, waits for them, and re-layouts  6.82 us (9%)
  between operations  0.83 us (1%)
    pallas_call x1, Pallas kernels, couple(): pl.pallas_call(kernel, out_shape=jax.ShapeDtypeStruct((64, 3072), BF16),...  67.3 us
    reshape x1, local copies, waits for them, and re-layouts, body(): columns = coupling.reshape(25, 2, 128, 48).transpose(3, 1, 0, 2)  3.04 us
    unnamed x13, local copies, waits for them, and re-layouts  1.57 us

profile of v1, /device:TPU:1, one launch (start us, length us, event | category | flops | bytes accessed | tf_op | source)
XLA Modules:
  0.0 75.2 jit_solution(10185729887897348304)
XLA Ops:
  0.0 3.0 %reshape.31 = bf16[25,2,128,48]{3,2,1,0:T(8,128)(2,1)S(1)} reshape(bf16[25,2,6144]{2,1,0:T(2,128)(2,1)} %param.7) | data formatting | bytes 1228800 | tf_op jit(solution)/shard_map/reshape | solution.py:295
  3.0 0.0 copy-start
  3.1 1.4 %copy.17 = bf16[48,2,25,128]{3,2,1,0:T(8,128)(2,1)S(1)} copy(bf16[48,2,25,128]{0,3,1,2:T(8,128)(2,1)S(1)} %bitcast.19) | data formatting | bytes 1228800
  4.4 0.0 copy-start.2
  4.4 0.0 copy-start.3
  4.5 0.0 copy-start.4
  4.5 0.0 copy-start.1
  4.5 0.1 pad.8.clone
  4.6 0.0 copy-done
  4.6 0.1 slice_reduce_fusion
  4.7 0.1 squeeze.7
  4.8 0.1 squeeze.6
  4.9 0.1 maximum_bitcast_fusion
  5.0 0.1 reduce.2
  5.1 0.1 reshape_reshape.3
  5.2 0.1 copy.16.eig_ref
  5.9 0.0 copy-done.2
  5.9 0.1 copy.14
  6.0 0.0 copy-done.3
  6.0 0.1 copy.15
  6.1 0.0 copy-done.4
  6.1 0.1 broadcast_in_dim.28
  6.2 0.1 broadcast_in_dim.29
  6.3 0.0 copy-done.1
  6.3 0.1 reshape.34
  6.4 0.1 reshape.35
  6.6 0.1 pad.12.clone
  6.7 0.1 maximum_maximum_fusion.lat_ref
  6.7 67.3 %couple.1 = bf16[64,3072]{1,0:T(8,128)(2,1)S(1)} custom-call(bf16[16,3,64,128]{3,2,1,0:T(8,128)(2,1)S(1)} %bitcast.16, bf16[2,64,128]{2,1,0:T(8,128)(2,1)S(1)} %pad_maximum_fusion.near_ref, bf16[64,128]{1,0:T(8,128)(2,1)S(1)} %copy.16.eig_ref, s32[8,128]{1,0:T(8,128)S(1)} %broadcast_in_dim.25.part_ref, f32[32,3]{1,0:T(8,128)S(1)} %bitcast.17, ...), custom_call_target="tpu_custom_call" | custom-call | tf_op jit(solution)/shard_map/couple/pallas_call | solution.py:258
  74.0 1.2 %reshape.36 = bf16[1,1,196608]{2,1,0:T(2,128)(2,1)} reshape(bf16[64,3072]{1,0:T(8,128)(2,1)S(1)} %couple.1) | data formatting | bytes 786432 | tf_op jit(solution)/shard_map/reshape | solution.py:307
  (7 shorter events, 0.1 us)
Async XLA Ops:
  3.0 1.5 %copy-start = (bf16[1,8192]{1,0:T(2,128)(2,1)S(1)}, bf16[1,8192]{1,0:T(2,128)(2,1)}, u32[]{:S(2)}) copy-start(bf16[1,8192]{1,0:T(2,128)(2,1)} %param.8) | copy-start | bytes 49156
  4.4 1.5 %copy-start.2 = (f32[3,32]{1,0:T(4,128)S(1)}, f32[3,32]{1,0:T(4,128)}, u32[]{:S(2)}) copy-start(f32[3,32]{1,0:T(4,128)} %param.10) | copy-start | bytes 1156
  4.4 1.6 %copy-start.3 = (f32[3,16]{1,0:T(4,128)S(1)}, f32[3,16]{1,0:T(4,128)}, u32[]{:S(2)}) copy-start(f32[3,16]{1,0:T(4,128)} %param.11) | copy-start | bytes 580
  4.5 1.7 %copy-start.4 = (f32[2]{0:T(128)S(1)}, f32[2]{0:T(128)}, u32[]{:S(2)}) copy-start(f32[2]{0:T(128)} %constant.8.clone) | copy-start | bytes 28
  4.5 1.8 %copy-start.1 = (s32[6,400]{1,0:T(8,128)S(1)}, s32[6,400]{1,0:T(8,128)}, u32[]{:S(2)}) copy-start(s32[6,400]{1,0:T(8,128)} %param.12) | copy-start | bytes 28804

commit v2 on v1

--- a/solution.py
+++ b/solution.py
@@ -48,6 +48,74 @@
 
     own = pltpu.make_async_copy(c_hbm.at[pb], cols.at[:, pb], own_sem)
     own.start()
+
+    with jax.named_scope("entry"):
+        pl.semaphore_wait(barrier, NPB - 1 + NKA - 1)
+
+    def c_copy(v, step):
+        to = pb_peer(step)
+        return pltpu.make_async_remote_copy(
+            src_ref=c_hbm.at[to, v], dst_ref=cols.at[v, pb],
+            send_sem=c_ss.at[v], recv_sem=c_rs.at[v],
+            device_id=(to, ka), device_id_type=MESH,
+        )
+
+    def z_copy(step):
+        other = lax.rem(zi + step, NZ)
+        return pltpu.make_async_remote_copy(
+            src_ref=eig_ref, dst_ref=table.at[xi, zi],
+            send_sem=z_ss, recv_sem=z_rs,
+            device_id=(pb, other * NX + xi), device_id_type=MESH,
+        )
+
+    def x_copy(step):
+        other = lax.rem(xi + step, NX)
+        return pltpu.make_async_remote_copy(
+            src_ref=table.at[xi], dst_ref=table.at[xi],
+            send_sem=x_ss, recv_sem=x_rs,
+            device_id=(pb, zi * NX + other), device_id_type=MESH,
+        )
+
+    def p_copy(step):
+        other = pb_peer(step)
+        return pltpu.make_async_remote_copy(
+            src_ref=part_ref, dst_ref=parts.at[pb],
+            send_sem=p_ss, recv_sem=p_rs,
+            device_id=(other, ka), device_id_type=MESH,
+        )
+
+    def b_copy(v, step):
+        other = ka_peer(step)
+        return pltpu.make_async_remote_copy(
+            src_ref=bsend.at[v, other], dst_ref=brecv.at[v, ka],
+            send_sem=b_ss.at[v], recv_sem=b_rs.at[v],
+            device_id=(pb, other), device_id_type=MESH,
+        )
+
+    def q_copy(v, step):
+        other = pb_peer(step)
+        return pltpu.make_async_remote_copy(
+            src_ref=qsend.at[v, other], dst_ref=qrecv.at[v, pb],
+            send_sem=q_ss.at[v], recv_sem=q_rs.at[v],
+            device_id=(other, ka), device_id_type=MESH,
+        )
+
+    def wait_all(ref, count, sem):
+        part = ref.at[pl.ds(0, count)]
+        pltpu.make_async_copy(part, part, sem).wait()
+
+    def loop(first, last, do):
+        def step_of(step, carry):
+            do(step)
+            return carry
+
+        lax.fori_loop(first, last, step_of, 0)
+
+    loop(1, NPB, lambda s: c_copy(0, s).start())
+    loop(1, NZ, lambda s: z_copy(s).start())
+    loop(1, NPB, lambda s: c_copy(1, s).start())
+    loop(1, NPB, lambda s: c_copy(2, s).start())
+    loop(1, NPB, lambda s: p_copy(s).start())
 
     def turn(points, first, extra):
         t = extra
@@ -73,82 +141,6 @@
         wmat[rows0, lanes1] = -near_ref[1]
         wmat[rows1, lanes1] = near_ref[0]
 
-    pl.semaphore_wait(barrier, NPB - 1 + NKA - 1)
-
-    def c_copy(v, step):
-        to = pb_peer(step)
-        return pltpu.make_async_remote_copy(
-            src_ref=c_hbm.at[to, v], dst_ref=cols.at[v, pb],
-            send_sem=c_ss.at[v, to], recv_sem=c_rs.at[v, pb],
-            device_id=(to, ka), device_id_type=MESH,
-        )
-
-    def c_recv(v, step):
-        src = pb_peer(step)
-        return pltpu.make_async_remote_copy(
-            src_ref=c_hbm.at[src, v], dst_ref=cols.at[v, src],
-            send_sem=c_ss.at[v, src], recv_sem=c_rs.at[v, src],
-            device_id=(src, ka), device_id_type=MESH,
-        )
-
-    def z_copy(step, sending):
-        other = lax.rem(zi + step, NZ)
-        slot = zi if sending else other
-        return pltpu.make_async_remote_copy(
-            src_ref=eig_ref, dst_ref=table.at[xi, slot],
-            send_sem=z_ss.at[other], recv_sem=z_rs.at[slot],
-            device_id=(pb, other * NX + xi), device_id_type=MESH,
-        )
-
-    def x_copy(step, sending):
-        other = lax.rem(xi + step, NX)
-        slot = xi if sending else other
-        return pltpu.make_async_remote_copy(
-            src_ref=table.at[slot], dst_ref=table.at[slot],
-            send_sem=x_ss.at[other], recv_sem=x_rs.at[slot],
-            device_id=(pb, zi * NX + other), device_id_type=MESH,
-        )
-
-    def p_copy(step, sending):
-        other = pb_peer(step)
-        slot = pb if sending else other
-        return pltpu.make_async_remote_copy(
-            src_ref=part_ref, dst_ref=parts.at[slot],
-            send_sem=p_ss.at[other], recv_sem=p_rs.at[slot],
-            device_id=(other, ka), device_id_type=MESH,
-        )
-
-    def b_copy(v, step, sending):
-        other = ka_peer(step)
-        slot = ka if sending else other
-        return pltpu.make_async_remote_copy(
-            src_ref=bsend.at[v, other], dst_ref=brecv.at[v, slot],
-            send_sem=b_ss.at[v, other], recv_sem=b_rs.at[v, slot],
-            device_id=(pb, other), device_id_type=MESH,
-        )
-
-    def q_copy(v, step, sending):
-        other = pb_peer(step)
-        slot = pb if sending else other
-        return pltpu.make_async_remote_copy(
-            src_ref=qsend.at[v, other], dst_ref=qrecv.at[v, slot],
-            send_sem=q_ss.at[v, other], recv_sem=q_rs.at[v, slot],
-            device_id=(other, ka), device_id_type=MESH,
-        )
-
-    def loop(first, last, do):
-        def step_of(step, carry):
-            do(step)
-            return carry
-
-        lax.fori_loop(first, last, step_of, 0)
-
-    loop(1, NPB, lambda s: c_copy(0, s).start())
-    loop(1, NZ, lambda s: z_copy(s, True).start())
-    loop(1, NPB, lambda s: c_copy(1, s).start())
-    loop(1, NPB, lambda s: c_copy(2, s).start())
-    loop(1, NPB, lambda s: p_copy(s, True).start())
-
     table[xi, zi] = eig_ref[...]
     parts[pb] = part_ref[...]
 
@@ -158,15 +150,18 @@
         phase[k, 0:16, :] = (c * cq[...] - s * sq[...]).astype(BF16)
         phase[k, 16:32, :] = (s * cq[...] + c * sq[...]).astype(BF16)
 
-    loop(0, NKA, make_phase)
-
-    loop(1, NZ, lambda s: z_copy(s, False).wait_recv())
-    loop(1, NX, lambda s: x_copy(s, True).start())
+    with jax.named_scope("phases"):
+        loop(0, NKA, make_phase)
+
+    with jax.named_scope("vectors_wait"):
+        wait_all(table.at[0], NZ - 1, z_rs)
+        loop(1, NX, lambda s: x_copy(s).start())
 
     own.wait()
 
     def bloch_of(v):
-        loop(1, NPB, lambda s: c_recv(v, s).wait_recv())
+        with jax.named_scope("couplings_wait"):
+            wait_all(cols.at[v], NPB - 1, c_rs.at[v])
 
         def part(n):
             rows = pl.ds(n * 8, 8)
@@ -176,14 +171,17 @@
             )
             bsend[v, rows] = got.astype(BF16).reshape(8, 32, 128)
 
-        loop(0, 4, part)
-        loop(1, NKA, lambda s: b_copy(v, s, True).start())
+        with jax.named_scope("bloch"):
+            loop(0, 4, part)
+        with jax.named_scope("bloch_send"):
+            loop(1, NKA, lambda s: b_copy(v, s).start())
         brecv[v, ka] = bsend[v, ka]
 
     loop(0, VS, bloch_of)
 
-    loop(1, NX, lambda s: x_copy(s, False).wait_recv())
-    loop(1, NPB, lambda s: p_copy(s, False).wait_recv())
+    with jax.named_scope("vectors_wait_x"):
+        wait_all(table, NX - 1, x_rs)
+        wait_all(parts, NPB - 1, p_rs)
 
     low = lax.broadcasted_iota(jnp.int32, (32, 128), 1) < 64
 
@@ -201,7 +199,8 @@
         return jnp.where(low, both[0:32], both[32:64]).astype(BF16)
 
     def rotate(v):
-        loop(1, NKA, lambda s: b_copy(v, s, False).wait_recv())
+        with jax.named_scope("bloch_wait"):
+            wait_all(brecv.at[v], NKA - 1, b_rs.at[v])
 
         def near(n):
             rows = pl.ds(n * 8, 8)
@@ -213,20 +212,30 @@
             for t in range(4):
                 tmat[t, pl.ds(n * 128, 128), :] = got[:, t * 128 : (t + 1) * 128]
 
-        loop(0, 4, near)
-
-        def one(s):
-            q = pb_peer(s)
-            qsend[v, q] = squares(q)
-            q_copy(v, s, True).start()
-
-        loop(1, NPB, one)
-        qrecv[v, pb] = squares(pb)
+        with jax.named_scope("near_rotation"):
+            loop(0, 4, near)
+
+        def four(n):
+            for s in range(4):
+                q = pb_peer(4 * n + s)
+                qsend[v, q] = squares(q)
+
+            def send(s):
+                @pl.when(s > 0)
+                def _():
+                    q_copy(v, s).start()
+
+            loop(4 * n, 4 * n + 4, send)
+
+        with jax.named_scope("far_rotation"):
+            loop(0, 4, four)
+        qrecv[v, pb] = qsend[v, pb]
 
     loop(0, VS, rotate)
 
     def place(v):
-        loop(1, NPB, lambda s: q_copy(v, s, False).wait_recv())
+        with jax.named_scope("squares_wait"):
+            wait_all(qrecv.at[v], NPB - 1, q_rs.at[v])
 
         def one(s):
             spread[pl.ds(3 * s + v, 32, stride=48), :] = qrecv[v, s].astype(F32)
@@ -235,21 +244,23 @@
 
     loop(0, VS, place)
 
-    for n in range(12):
-        block = spread[n * 128 : (n + 1) * 128, :].T.astype(BF16)
-        out_ref[:, n * 128 : (n + 1) * 128] = block[0:64]
-        out_ref[:, 1536 + n * 128 : 1536 + (n + 1) * 128] = block[64:128]
-
-    loop(1, NZ, lambda s: z_copy(s, True).wait_send())
-    loop(1, NX, lambda s: x_copy(s, True).wait_send())
-    loop(1, NPB, lambda s: p_copy(s, True).wait_send())
-
-    def drain(v):
-        loop(1, NPB, lambda s: c_copy(v, s).wait_send())
-        loop(1, NKA, lambda s: b_copy(v, s, True).wait_send())
-        loop(1, NPB, lambda s: q_copy(v, s, True).wait_send())
-
-    loop(0, VS, drain)
+    with jax.named_scope("output"):
+        for n in range(12):
+            block = spread[n * 128 : (n + 1) * 128, :].T.astype(BF16)
+            out_ref[:, n * 128 : (n + 1) * 128] = block[0:64]
+            out_ref[:, 1536 + n * 128 : 1536 + (n + 1) * 128] = block[64:128]
+
+    with jax.named_scope("drain"):
+        wait_all(table.at[0], NZ - 1, z_ss)
+        wait_all(table, NX - 1, x_ss)
+        wait_all(parts, NPB - 1, p_ss)
+
+        def drain(v):
+            wait_all(cols.at[v], NPB - 1, c_ss.at[v])
+            wait_all(bsend.at[v], NKA - 1, b_ss.at[v])
+            wait_all(qsend.at[v], NPB - 1, q_ss.at[v])
+
+        loop(0, VS, drain)
 
 
 def couple(columns, near, eig, part, kp, qp, lat):
@@ -276,12 +287,12 @@
             pltpu.VMEM((VS, NPB, 32, 128), BF16),
             pltpu.VMEM((VS, NPB, 32, 128), BF16),
             pltpu.VMEM((1536, 128), F32),
-            dma((VS, NPB)), dma((VS, NPB)),
-            dma((VS, NKA)), dma((VS, NKA)),
-            dma((VS, NPB)), dma((VS, NPB)),
-            dma((NZ,)), dma((NZ,)),
-            dma((NX,)), dma((NX,)),
-            dma((NPB,)), dma((NPB,)),
+            dma((VS,)), dma((VS,)),
+            dma((VS,)), dma((VS,)),
+            dma((VS,)), dma((VS,)),
+            dma(()), dma(()),
+            dma(()), dma(()),
+            dma(()), dma(()),
             dma(()),
         ],
         compiler_params=pltpu.CompilerParams(

time: 75.3 us -> 64.1 us (0.85)
  Pallas kernels: 67.3 us -> 56 us
    pallas_call x1, Pallas kernels: 67.3 us -> 56 us  [couple(): pl.pallas_call(kernel, out_shape=jax.ShapeDtypeStruct((64, 3072), BF16),...]
where the time goes in v2:
time: 64.1 us; the launch traced here: 63.9 us
  Pallas kernels  56 us (87%)
  local copies, waits for them, and re-layouts  6.82 us (11%)
  between operations  0.83 us (1%)
    pallas_call x1, Pallas kernels, couple(): pl.pallas_call(kernel, out_shape=jax.ShapeDtypeStruct((64, 3072), BF16),...  56 us
    reshape x1, local copies, waits for them, and re-layouts, body(): columns = coupling.reshape(25, 2, 128, 48).transpose(3, 1, 0, 2)  3.04 us
    unnamed x13, local copies, waits for them, and re-layouts  1.57 us

profile of v2, /device:TPU:1, one launch (start us, length us, event | category | flops | bytes accessed | tf_op | source)
XLA Modules:
  0.0 63.9 jit_solution(3052926553095664679)
XLA Ops:
  0.0 3.0 %reshape.31 = bf16[25,2,128,48]{3,2,1,0:T(8,128)(2,1)S(1)} reshape(bf16[25,2,6144]{2,1,0:T(2,128)(2,1)} %param.7) | data formatting | bytes 1228800 | tf_op jit(solution)/shard_map/reshape | solution.py:306
  3.0 0.0 copy-start
  3.1 1.4 %copy.17 = bf16[48,2,25,128]{3,2,1,0:T(8,128)(2,1)S(1)} copy(bf16[48,2,25,128]{0,3,1,2:T(8,128)(2,1)S(1)} %bitcast.19) | data formatting | bytes 1228800
  4.4 0.0 copy-start.2
  4.4 0.0 copy-start.3
  4.5 0.0 copy-start.4
  4.5 0.0 copy-start.1
  4.5 0.1 pad.8.clone
  4.6 0.0 copy-done
  4.6 0.1 slice_reduce_fusion
  4.7 0.1 squeeze.7
  4.8 0.1 squeeze.6
  4.9 0.1 maximum_bitcast_fusion
  5.0 0.1 reduce.2
  5.1 0.1 reshape_reshape.3
  5.2 0.1 copy.16.eig_ref
  5.9 0.0 copy-done.2
  5.9 0.1 copy.14
  6.0 0.0 copy-done.3
  6.0 0.1 copy.15
  6.1 0.0 copy-done.4
  6.1 0.1 broadcast_in_dim.28
  6.2 0.1 broadcast_in_dim.29
  6.3 0.0 copy-done.1
  6.3 0.1 reshape.34
  6.4 0.1 reshape.35
  6.6 0.1 pad.12.clone
  6.7 0.1 maximum_maximum_fusion.lat_ref
  6.7 56.0 %couple.1 = bf16[64,3072]{1,0:T(8,128)(2,1)S(1)} custom-call(bf16[16,3,64,128]{3,2,1,0:T(8,128)(2,1)S(1)} %bitcast.16, bf16[2,64,128]{2,1,0:T(8,128)(2,1)S(1)} %pad_maximum_fusion.near_ref, bf16[64,128]{1,0:T(8,128)(2,1)S(1)} %copy.16.eig_ref, s32[8,128]{1,0:T(8,128)S(1)} %broadcast_in_dim.25.part_ref, f32[32,3]{1,0:T(8,128)S(1)} %bitcast.17, ...), custom_call_target="tpu_custom_call" | custom-call | tf_op jit(solution)/shard_map/couple/pallas_call | solution.py:269
  62.8 1.2 %reshape.36 = bf16[1,1,196608]{2,1,0:T(2,128)(2,1)} reshape(bf16[64,3072]{1,0:T(8,128)(2,1)S(1)} %couple.1) | data formatting | bytes 786432 | tf_op jit(solution)/shard_map/reshape | solution.py:318
  (7 shorter events, 0.1 us)
Async XLA Ops:
  3.0 1.5 %copy-start = (bf16[1,8192]{1,0:T(2,128)(2,1)S(1)}, bf16[1,8192]{1,0:T(2,128)(2,1)}, u32[]{:S(2)}) copy-start(bf16[1,8192]{1,0:T(2,128)(2,1)} %param.8) | copy-start | bytes 49156
  4.4 1.5 %copy-start.2 = (f32[3,32]{1,0:T(4,128)S(1)}, f32[3,32]{1,0:T(4,128)}, u32[]{:S(2)}) copy-start(f32[3,32]{1,0:T(4,128)} %param.10) | copy-start | bytes 1156
  4.4 1.6 %copy-start.3 = (f32[3,16]{1,0:T(4,128)S(1)}, f32[3,16]{1,0:T(4,128)}, u32[]{:S(2)}) copy-start(f32[3,16]{1,0:T(4,128)} %param.11) | copy-start | bytes 580
  4.5 1.7 %copy-start.4 = (f32[2]{0:T(128)S(1)}, f32[2]{0:T(128)}, u32[]{:S(2)}) copy-start(f32[2]{0:T(128)} %constant.8.clone) | copy-start | bytes 28
  4.5 1.8 %copy-start.1 = (s32[6,400]{1,0:T(8,128)S(1)}, s32[6,400]{1,0:T(8,128)}, u32[]{:S(2)}) copy-start(s32[6,400]{1,0:T(8,128)} %param.12) | copy-start | bytes 28804

commit v3 on v2

--- a/solution.py
+++ b/solution.py
@@ -18,9 +18,10 @@
 
 
 def kernel(
-    c_hbm, near_ref, eig_ref, part_ref, kp_ref, qp_ref, lat_ref, out_ref,
-    ck, sk, cq, sq, phase, wmat, cols, bsend, brecv, table, parts, tmat, qsend, qrecv, spread,
-    c_ss, c_rs, b_ss, b_rs, q_ss, q_rs, z_ss, z_rs, x_ss, x_rs, p_ss, p_rs, own_sem,
+    c_ref, vec_ref, part_ref, kp_ref, qp_ref, lat_ref, out_ref,
+    turned, rest, csend, esend, erecv, cols, points, lat, vecs, eig, part,
+    ck, sk, cq, sq, phase, wmat, bsend, brecv, table, parts, tmat, qsend, qrecv, spread,
+    c_ss, c_rs, e_ss, e_rs, b_ss, b_rs, q_ss, q_rs, z_ss, z_rs, x_ss, x_rs, p_ss, p_rs,
 ):
     pb = lax.axis_index("pb")
     ka = lax.axis_index("ka")
@@ -46,24 +47,26 @@
     lax.fori_loop(1, NPB, greet_pb, 0)
     lax.fori_loop(1, NKA, greet_ka, 0)
 
-    own = pltpu.make_async_copy(c_hbm.at[pb], cols.at[:, pb], own_sem)
-    own.start()
-
-    with jax.named_scope("entry"):
-        pl.semaphore_wait(barrier, NPB - 1 + NKA - 1)
-
     def c_copy(v, step):
         to = pb_peer(step)
         return pltpu.make_async_remote_copy(
-            src_ref=c_hbm.at[to, v], dst_ref=cols.at[v, pb],
+            src_ref=csend.at[v, to], dst_ref=cols.at[v, pl.ds(pl.multiple_of(pb * 48, 16), 48)],
             send_sem=c_ss.at[v], recv_sem=c_rs.at[v],
             device_id=(to, ka), device_id_type=MESH,
         )
 
+    def e_copy(step):
+        to = pb_peer(step)
+        return pltpu.make_async_remote_copy(
+            src_ref=esend.at[to], dst_ref=erecv.at[pb],
+            send_sem=e_ss, recv_sem=e_rs,
+            device_id=(to, ka), device_id_type=MESH,
+        )
+
     def z_copy(step):
         other = lax.rem(zi + step, NZ)
         return pltpu.make_async_remote_copy(
-            src_ref=eig_ref, dst_ref=table.at[xi, zi],
+            src_ref=eig, dst_ref=table.at[xi, zi],
             send_sem=z_ss, recv_sem=z_rs,
             device_id=(pb, other * NX + xi), device_id_type=MESH,
         )
@@ -79,7 +82,7 @@
     def p_copy(step):
         other = pb_peer(step)
         return pltpu.make_async_remote_copy(
-            src_ref=part_ref, dst_ref=parts.at[pb],
+            src_ref=part, dst_ref=parts.at[pb],
             send_sem=p_ss, recv_sem=p_rs,
             device_id=(other, ka), device_id_type=MESH,
         )
@@ -111,38 +114,106 @@
 
         lax.fori_loop(first, last, step_of, 0)
 
+    low = lax.broadcasted_iota(jnp.int32, (32, 128), 1) < 64
+    low64 = lax.broadcasted_iota(jnp.int32, (64, 128), 1) < 64
+    line = lax.broadcasted_iota(jnp.int32, (128, 128), 0)
+    unit = (line == lax.broadcasted_iota(jnp.int32, (128, 128), 1)).astype(BF16)
+
+    def flip(block):
+        return lax.dot_general(unit, block, (((1,), (1,)), ((), ())), preferred_element_type=F32)
+
+    def turn_four(n):
+        for t in range(4):
+            first = pl.multiple_of((4 * n + t) * 128, 128)
+            second = pl.multiple_of(3072 + (4 * n + t) * 128, 128)
+            both = jnp.concatenate([c_ref[:, pl.ds(first, 128)], c_ref[:, pl.ds(second, 128)]], axis=0)
+            turned[pl.ds(first, 128), :] = flip(both)
+
+    def pick(v):
+        def four(n):
+            for t in range(4):
+                to = 4 * n + t
+                field = turned[pl.ds(3 * to + v, 64, stride=48), :].astype(BF16)
+                got = flip(jnp.concatenate([field, field], axis=0))
+                got = jnp.where(low64, got[0:64], got[64:128])
+                csend[v, to] = got[0:48].astype(BF16)
+                rest[to, 2 * v : 2 * v + 2, :] = got[48:50]
+
+        loop(0, 4, four)
+        cols[v, pl.ds(pl.multiple_of(pb * 48, 16), 48)] = csend[v, pb]
+
+    rest[...] = jnp.zeros_like(rest)
+    with jax.named_scope("transpose"):
+        loop(0, 6, turn_four)
+    with jax.named_scope("pick"):
+        pick(0)
+
+    with jax.named_scope("entry"):
+        pl.semaphore_wait(barrier, NPB - 1 + NKA - 1)
+
     loop(1, NPB, lambda s: c_copy(0, s).start())
-    loop(1, NZ, lambda s: z_copy(s).start())
+    with jax.named_scope("pick"):
+        pick(1)
+        pick(2)
+    esend[...] = rest[...].astype(BF16)
+    erecv[pb] = esend[pb]
+    loop(1, NPB, lambda s: e_copy(s).start())
     loop(1, NPB, lambda s: c_copy(1, s).start())
     loop(1, NPB, lambda s: c_copy(2, s).start())
-    loop(1, NPB, lambda s: p_copy(s).start())
-
-    def turn(points, first, extra):
-        t = extra
+
+    with jax.named_scope("vectors"):
+        vectors = vec_ref[...]
+        vecs[...] = jnp.concatenate([vectors, vectors], axis=1).astype(F32)
+        lines = [vecs[pl.ds(64 * c + i2, 32, stride=2), :] for c in range(2) for i2 in range(2)]
+        eig[...] = jnp.concatenate(lines, axis=0).T[0:64].astype(BF16)
+        table[xi, zi] = eig[...]
+        loop(1, NZ, lambda s: z_copy(s).start())
+        part[...] = jnp.full((8, 128), part_ref[0, 0], jnp.int32)
+        parts[pb] = part[...]
+        loop(1, NPB, lambda s: p_copy(s).start())
+
+    def turn(where, first, rows):
+        points[...] = jnp.zeros_like(points)
+        points[0:3, 0 : where.shape[1]] = where[...]
+        across = points[...].T
+        t = jnp.zeros((rows, 1024), F32)
         for axis in range(3):
-            t = t + points[:, axis : axis + 1] * lat_ref[first + axis : first + axis + 1, :]
-        return (2.0 * math.pi) * (t - jnp.round(t))
-
-    ang = turn(kp_ref[...], 0, jnp.zeros((NKA, 1024), F32))
-    ck[...] = jnp.cos(ang)
-    sk[...] = jnp.sin(ang)
-    ang = turn(qp_ref[...], 3, jnp.broadcast_to(lat_ref[6:7, :], (NPB, 1024)))
-    cq[...] = jnp.cos(ang)
-    sq[...] = jnp.sin(ang)
-
+            t = t + across[0:rows, axis : axis + 1] * spots[first + axis : first + axis + 1, :]
+        return t
+
+    with jax.named_scope("tables"):
+        lane = lax.broadcasted_iota(jnp.int32, (1, 1024), 1)
+        source = lax.shift_right_logical(lane * 1366, 16)
+        pair = lax.shift_right_logical(lane - 48 * source, 1)
+        extra = 25 * lax.shift_right_logical(lane - 768, 4) + 24
+        pair = jnp.where(lane < 768, 25 * source + pair, extra)
+        quarter = jnp.where(lax.bitwise_and(lane, 1) == 1, 0.25, 0.0)
+        lat[...] = jnp.zeros_like(lat)
+        lat[0:6, 0:400] = lat_ref[...].astype(F32)
+        chosen = (lax.broadcasted_iota(jnp.int32, (512, 1024), 0) == pair).astype(BF16)
+        spots = jnp.dot(lat[...].astype(BF16), chosen, preferred_element_type=F32)
+        ang = turn(kp_ref, 0, NKA)
+        ang = (2.0 * math.pi) * (ang - jnp.round(ang))
+        ck[...] = jnp.cos(ang)
+        sk[...] = jnp.sin(ang)
+        ang = turn(qp_ref, 3, NPB) + quarter
+        ang = (2.0 * math.pi) * (ang - jnp.round(ang))
+        cq[...] = jnp.cos(ang)
+        sq[...] = jnp.sin(ang)
+
+    real, imag = vectors[0:64], vectors[64:128]
+    near0 = jnp.concatenate([real, imag], axis=1)
+    near1 = jnp.concatenate([-imag, real], axis=1)
     wmat[...] = jnp.zeros_like(wmat)
     for i2 in range(2):
         rows0 = pl.ds(i2 * 64, 64)
         rows1 = pl.ds(128 + i2 * 64, 64)
         lanes0 = pl.ds(i2 * 128, 128)
         lanes1 = pl.ds(256 + i2 * 128, 128)
-        wmat[rows0, lanes0] = near_ref[0]
-        wmat[rows1, lanes0] = near_ref[1]
-        wmat[rows0, lanes1] = -near_ref[1]
-        wmat[rows1, lanes1] = near_ref[0]
-
-    table[xi, zi] = eig_ref[...]
-    parts[pb] = part_ref[...]
+        wmat[rows0, lanes0] = near0
+        wmat[rows1, lanes0] = near1
+        wmat[rows0, lanes1] = -near1
+        wmat[rows1, lanes1] = near0
 
     def make_phase(k):
         c = ck[pl.ds(k, 1), :]
@@ -157,16 +228,22 @@
         wait_all(table.at[0], NZ - 1, z_rs)
         loop(1, NX, lambda s: x_copy(s).start())
 
-    own.wait()
+    with jax.named_scope("rest_wait"):
+        wait_all(erecv, NPB - 1, e_rs)
+
+    which = lax.shift_right_logical(lax.broadcasted_iota(jnp.int32, (NPB, 16, 128), 1), 1)
 
     def bloch_of(v):
         with jax.named_scope("couplings_wait"):
-            wait_all(cols.at[v], NPB - 1, c_rs.at[v])
+            arrived = cols.at[v, pl.ds(0, 48 * (NPB - 1))]
+            pltpu.make_async_copy(arrived, arrived, c_rs.at[v]).wait()
+        last = jnp.where(which == v, erecv[...].astype(F32), 0.0).astype(BF16)
+        cols[v, 768:1024] = last.reshape(256, 128)
 
         def part(n):
             rows = pl.ds(n * 8, 8)
             got = jnp.dot(
-                phase[rows].reshape(256, 1024), cols[v].reshape(1024, 128),
+                phase[rows].reshape(256, 1024), cols[v],
                 preferred_element_type=F32,
             )
             bsend[v, rows] = got.astype(BF16).reshape(8, 32, 128)
@@ -182,8 +259,6 @@
     with jax.named_scope("vectors_wait_x"):
         wait_all(table, NX - 1, x_rs)
         wait_all(parts, NPB - 1, p_rs)
-
-    low = lax.broadcasted_iota(jnp.int32, (32, 128), 1) < 64
 
     def squares(q):
         field = jnp.concatenate([tmat[t, pl.ds(q, 32, stride=16), :] for t in range(4)], axis=0)
@@ -254,31 +329,42 @@
         wait_all(table.at[0], NZ - 1, z_ss)
         wait_all(table, NX - 1, x_ss)
         wait_all(parts, NPB - 1, p_ss)
+        wait_all(esend, NPB - 1, e_ss)
 
         def drain(v):
-            wait_all(cols.at[v], NPB - 1, c_ss.at[v])
+            wait_all(csend.at[v], NPB - 1, c_ss.at[v])
             wait_all(bsend.at[v], NKA - 1, b_ss.at[v])
             wait_all(qsend.at[v], NPB - 1, q_ss.at[v])
 
         loop(0, VS, drain)
 
 
-def couple(columns, near, eig, part, kp, qp, lat):
+def couple(columns, vectors, part, kp, qp, lat):
     vmem = pl.BlockSpec(memory_space=pltpu.VMEM)
     dma = pltpu.SemaphoreType.DMA
     return pl.pallas_call(
         kernel,
         out_shape=jax.ShapeDtypeStruct((64, 3072), BF16),
-        in_specs=[pl.BlockSpec(memory_space=pl.ANY)] + [vmem] * 6,
+        in_specs=[vmem, vmem, pl.BlockSpec(memory_space=pltpu.SMEM), vmem, vmem, vmem],
         out_specs=vmem,
         scratch_shapes=[
+            pltpu.VMEM((3072, 128), F32),
+            pltpu.VMEM((NPB, 16, 128), F32),
+            pltpu.VMEM((VS, NPB, 48, 128), BF16),
+            pltpu.VMEM((NPB, 16, 128), BF16),
+            pltpu.VMEM((NPB, 16, 128), BF16),
+            pltpu.VMEM((VS, 1024, 128), BF16),
+            pltpu.VMEM((8, 128), F32),
+            pltpu.VMEM((8, 512), F32),
+            pltpu.VMEM((128, 128), F32),
+            pltpu.VMEM((64, 128), BF16),
+            pltpu.VMEM((8, 128), jnp.int32),
             pltpu.VMEM((NKA, 1024), F32),
             pltpu.VMEM((NKA, 1024), F32),
             pltpu.VMEM((NPB, 1024), F32),
             pltpu.VMEM((NPB, 1024), F32),
             pltpu.VMEM((NKA, 32, 1024), BF16),
             pltpu.VMEM((256, 512), BF16),
-            pltpu.VMEM((VS, NPB, 64, 128), BF16),
             pltpu.VMEM((VS, NKA, 32, 128), BF16),
             pltpu.VMEM((VS, NKA, 32, 128), BF16),
             pltpu.VMEM((NX, NZ, 64, 128), BF16),
@@ -288,33 +374,23 @@
             pltpu.VMEM((VS, NPB, 32, 128), BF16),
             pltpu.VMEM((1536, 128), F32),
             dma((VS,)), dma((VS,)),
+            dma(()), dma(()),
             dma((VS,)), dma((VS,)),
             dma((VS,)), dma((VS,)),
             dma(()), dma(()),
             dma(()), dma(()),
             dma(()), dma(()),
-            dma(()),
         ],
         compiler_params=pltpu.CompilerParams(
             collective_id=0, has_side_effects=True, vmem_limit_bytes=40 << 20
         ),
         name="couple",
-    )(columns, near, eig, part, kp, qp, lat)
+    )(columns, vectors, part, kp, qp, lat)
 
 
 def body(coupling, eigvecs, partner, kpoints, qpoints, lattice):
-    columns = coupling.reshape(25, 2, 128, 48).transpose(3, 1, 0, 2)
-    columns = jnp.pad(columns, ((0, 0), (0, 0), (0, 7), (0, 0))).reshape(NPB, VS, 64, 128)
-    vectors = eigvecs.reshape(2, 64, 64)
-    real, imag = vectors[0], vectors[1]
-    near = jnp.stack([jnp.concatenate([real, imag], 1), jnp.concatenate([-imag, real], 1)])
-    eig = vectors.reshape(2, 32, 2, 64).transpose(3, 0, 2, 1).reshape(64, 128)
-    part = jnp.broadcast_to(partner, (8, 128))
-    lat = jnp.pad(lattice.astype(F32).reshape(6, NPB, 1, 25), ((0, 0), (0, 0), (0, 0), (0, 7)))
-    lat = jnp.broadcast_to(lat, (6, NPB, 2, 32)).reshape(6, 1024)
-    quarter = jnp.broadcast_to(jnp.array([0.0, 0.25], F32).reshape(1, 1, 2, 1), (1, NPB, 2, 32))
-    lat = jnp.concatenate([lat, quarter.reshape(1, 1024), jnp.zeros((1, 1024), F32)], 0)
-    out = couple(columns, near, eig, part, kpoints.T, qpoints.T, lat)
+    columns = jnp.pad(coupling.reshape(50, 6144), ((0, 14), (0, 0)))
+    out = couple(columns, eigvecs.reshape(128, 64), partner, kpoints, qpoints, lattice)
     return out.reshape(1, 1, 196608)
 
 

time: 64.1 us -> 60.1 us (0.938)
  local copies, waits for them, and re-layouts: 6.82 us -> 4.1 us
  Pallas kernels: 56 us -> 55 us
    reshape x4 -> x2, local copies, waits for them, and re-layouts: 3.34 us -> 2.17 us  [the longest x1 2.09 us: body(): columns = jnp.pad(coupling.reshape(50, 6144), ((0, 14), (0, 0)))]
    pallas_call x1, Pallas kernels: 56 us -> 55 us  [couple(): pl.pallas_call(kernel, out_shape=jax.ShapeDtypeStruct((64, 3072), BF16),...]
    unnamed x13 -> x8, local copies, waits for them, and re-layouts: 1.57 us -> 0.71 us
where the time goes in v3:
time: 60.1 us; the launch traced here: 59.9 us
  Pallas kernels  55 us (92%)
  local copies, waits for them, and re-layouts  4.1 us (7%)
  between operations  0.73 us (1%)
    pallas_call x1, Pallas kernels, couple(): pl.pallas_call(kernel, out_shape=jax.ShapeDtypeStruct((64, 3072), BF16),...  55 us
    reshape x1, local copies, waits for them, and re-layouts, body(): columns = jnp.pad(coupling.reshape(50, 6144), ((0, 14), (0, 0)))  2.09 us

profile of v3, /device:TPU:1, one launch (start us, length us, event | category | flops | bytes accessed | tf_op | source)
XLA Modules:
  0.0 59.9 jit_solution(9318877519662379346)
XLA Ops:
  0.0 2.1 %reshape.9 = bf16[50,6144]{1,0:T(8,128)(2,1)S(1)} reshape(bf16[25,2,6144]{2,1,0:T(2,128)(2,1)} %param.6) | data formatting | bytes 1228800 | tf_op jit(solution)/shard_map/reshape | solution.py:392
  2.1 0.0 copy-start.3
  2.1 0.1 pad.4.c_ref
  2.2 0.7 %copy-done.3 = bf16[1,8192]{1,0:T(2,128)(2,1)S(1)} copy-done((bf16[1,8192]{1,0:T(2,128)(2,1)S(1)}, bf16[1,8192]{1,0:T(2,128)(2,1)}, u32[]{:S(2)}) %copy-start.3) | copy-done | bytes 16408
  2.9 0.1 reduce
  2.9 0.0 copy-start
  3.0 0.0 copy-start.1
  3.0 0.0 copy-start.2
  3.0 0.1 reshape.10.vec_ref
  3.7 0.0 copy-done
  3.7 0.0 copy-done.1
  3.7 0.0 copy-done.2
  3.7 55.0 %couple.1 = bf16[64,3072]{1,0:T(8,128)(2,1)S(1)} custom-call(bf16[64,6144]{1,0:T(8,128)(2,1)S(1)} %pad.4.c_ref, bf16[128,64]{1,0:T(8,128)(2,1)S(1)} %reshape.10.vec_ref, s32[1,1]{1,0:T(1,128)S(6)} %copy.7.part_ref, f32[3,32]{1,0:T(4,128)S(1)} %copy-done.1, f32[3,16]{1,0:T(4,128)S(1)} %copy-done.2, s32[6,400]{1,0:T(8,128)S(1)} %copy-done), custom_call_target="tpu_custom_call" | custom-call | tf_op jit(solution)/shard_map/couple/pallas_call | solution.py:345
  58.7 1.2 %reshape.11 = bf16[1,1,196608]{2,1,0:T(2,128)(2,1)} reshape(bf16[64,3072]{1,0:T(8,128)(2,1)S(1)} %couple.1) | data formatting | bytes 786432 | tf_op jit(solution)/shard_map/reshape | solution.py:394
Async XLA Ops:
  2.1 0.8 %copy-start.3 = (bf16[1,8192]{1,0:T(2,128)(2,1)S(1)}, bf16[1,8192]{1,0:T(2,128)(2,1)}, u32[]{:S(2)}) copy-start(bf16[1,8192]{1,0:T(2,128)(2,1)} %param.7) | copy-start | bytes 49156
  2.9 0.8 %copy-start = (s32[6,400]{1,0:T(8,128)S(1)}, s32[6,400]{1,0:T(8,128)}, u32[]{:S(2)}) copy-start(s32[6,400]{1,0:T(8,128)} %lat_ref.1) | copy-start | bytes 28804
  3.0 0.8 %copy-start.1 = (f32[3,32]{1,0:T(4,128)S(1)}, f32[3,32]{1,0:T(4,128)}, u32[]{:S(2)}) copy-start(f32[3,32]{1,0:T(4,128)} %kp_ref.1) | copy-start | bytes 1156
  3.0 0.8 %copy-start.2 = (f32[3,16]{1,0:T(4,128)S(1)}, f32[3,16]{1,0:T(4,128)}, u32[]{:S(2)}) copy-start(f32[3,16]{1,0:T(4,128)} %qp_ref.1) | copy-start | bytes 580

commit v4 on v3

--- a/solution.py
+++ b/solution.py
@@ -18,10 +18,10 @@
 
 
 def kernel(
-    c_ref, vec_ref, part_ref, kp_ref, qp_ref, lat_ref, out_ref,
-    turned, rest, csend, esend, erecv, cols, points, lat, vecs, eig, part,
+    c_hbm, vec_hbm, part_hbm, kp_hbm, qp_hbm, lat_hbm, out_ref,
+    c_ref, vec_ref, part_ref, kp_ref, qp_ref, lat_ref, turned, rest, csend, esend, erecv, cols, points, lat, vecs, lines, eig, part,
     ck, sk, cq, sq, phase, wmat, bsend, brecv, table, parts, tmat, qsend, qrecv, spread,
-    c_ss, c_rs, e_ss, e_rs, b_ss, b_rs, q_ss, q_rs, z_ss, z_rs, x_ss, x_rs, p_ss, p_rs,
+    c_ss, c_rs, e_ss, e_rs, b_ss, b_rs, q_ss, q_rs, z_ss, z_rs, x_ss, x_rs, p_ss, p_rs, in_sem,
 ):
     pb = lax.axis_index("pb")
     ka = lax.axis_index("ka")
@@ -34,6 +34,17 @@
     def ka_peer(step):
         return lax.rem(ka + step, NKA)
 
+    inputs = [
+        pltpu.make_async_copy(c_hbm, c_ref.at[pl.ds(0, 25)], in_sem.at[0]),
+        pltpu.make_async_copy(vec_hbm, vec_ref, in_sem.at[1]),
+        pltpu.make_async_copy(part_hbm, part_ref, in_sem.at[2]),
+        pltpu.make_async_copy(kp_hbm, kp_ref, in_sem.at[3]),
+        pltpu.make_async_copy(qp_hbm, qp_ref, in_sem.at[4]),
+        pltpu.make_async_copy(lat_hbm, lat_ref, in_sem.at[5]),
+    ]
+    for copy in inputs:
+        copy.start()
+
     barrier = pltpu.get_barrier_semaphore()
 
     def greet_pb(step, carry):
@@ -87,16 +98,14 @@
             device_id=(other, ka), device_id_type=MESH,
         )
 
-    def b_copy(v, step):
-        other = ka_peer(step)
-        return pltpu.make_async_remote_copy(
-            src_ref=bsend.at[v, other], dst_ref=brecv.at[v, ka],
-            send_sem=b_ss.at[v], recv_sem=b_rs.at[v],
+    def b_copy(v, h, other):
+        return pltpu.make_async_remote_copy(
+            src_ref=bsend.at[v, h, other], dst_ref=brecv.at[v, h, ka],
+            send_sem=b_ss.at[v, h], recv_sem=b_rs.at[v, h],
             device_id=(pb, other), device_id_type=MESH,
         )
 
-    def q_copy(v, step):
-        other = pb_peer(step)
+    def q_copy(v, other):
         return pltpu.make_async_remote_copy(
             src_ref=qsend.at[v, other], dst_ref=qrecv.at[v, pb],
             send_sem=q_ss.at[v], recv_sem=q_rs.at[v],
@@ -122,29 +131,34 @@
     def flip(block):
         return lax.dot_general(unit, block, (((1,), (1,)), ((), ())), preferred_element_type=F32)
 
-    def turn_four(n):
-        for t in range(4):
-            first = pl.multiple_of((4 * n + t) * 128, 128)
-            second = pl.multiple_of(3072 + (4 * n + t) * 128, 128)
-            both = jnp.concatenate([c_ref[:, pl.ds(first, 128)], c_ref[:, pl.ds(second, 128)]], axis=0)
+    def turn_some(n):
+        for t in range(8):
+            first = pl.multiple_of((8 * n + t) * 128, 128)
+            second = pl.multiple_of(3072 + (8 * n + t) * 128, 128)
+            both = jnp.concatenate(
+                [c_ref[:, :, pl.ds(first, 128)].reshape(64, 128), c_ref[:, :, pl.ds(second, 128)].reshape(64, 128)],
+                axis=0,
+            )
             turned[pl.ds(first, 128), :] = flip(both)
 
     def pick(v):
-        def four(n):
-            for t in range(4):
-                to = 4 * n + t
+        def some(n):
+            for t in range(8):
+                to = 8 * n + t
                 field = turned[pl.ds(3 * to + v, 64, stride=48), :].astype(BF16)
                 got = flip(jnp.concatenate([field, field], axis=0))
                 got = jnp.where(low64, got[0:64], got[64:128])
                 csend[v, to] = got[0:48].astype(BF16)
                 rest[to, 2 * v : 2 * v + 2, :] = got[48:50]
 
-        loop(0, 4, four)
+        loop(0, 2, some)
         cols[v, pl.ds(pl.multiple_of(pb * 48, 16), 48)] = csend[v, pb]
 
     rest[...] = jnp.zeros_like(rest)
+    c_ref[25:32] = jnp.zeros((7, 2, 6144), BF16)
+    inputs[0].wait()
     with jax.named_scope("transpose"):
-        loop(0, 6, turn_four)
+        loop(0, 3, turn_some)
     with jax.named_scope("pick"):
         pick(0)
 
@@ -162,23 +176,29 @@
     loop(1, NPB, lambda s: c_copy(2, s).start())
 
     with jax.named_scope("vectors"):
-        vectors = vec_ref[...]
-        vecs[...] = jnp.concatenate([vectors, vectors], axis=1).astype(F32)
-        lines = [vecs[pl.ds(64 * c + i2, 32, stride=2), :] for c in range(2) for i2 in range(2)]
-        eig[...] = jnp.concatenate(lines, axis=0).T[0:64].astype(BF16)
+        for copy in inputs[1:]:
+            copy.wait()
+        for t in range(64):
+            vecs[t : t + 1, :] = vec_ref[:, t * 128 : (t + 1) * 128].astype(F32)
+        across = jnp.concatenate([vecs[...], vecs[...]], axis=0).T
+        eig[...] = jnp.where(low64, across[0:64], across[64:128]).astype(BF16)
         table[xi, zi] = eig[...]
         loop(1, NZ, lambda s: z_copy(s).start())
-        part[...] = jnp.full((8, 128), part_ref[0, 0], jnp.int32)
+        part[...] = jnp.broadcast_to(part_ref[...], (8, 128))
         parts[pb] = part[...]
         loop(1, NPB, lambda s: p_copy(s).start())
 
-    def turn(where, first, rows):
+    def turn(where, first, order):
         points[...] = jnp.zeros_like(points)
         points[0:3, 0 : where.shape[1]] = where[...]
         across = points[...].T
-        t = jnp.zeros((rows, 1024), F32)
+        if order is None:
+            across = across[0:NKA]
+        else:
+            across = jnp.concatenate([across[q : q + 1] for q in order], axis=0)
+        t = jnp.zeros((across.shape[0], 1024), F32)
         for axis in range(3):
-            t = t + across[0:rows, axis : axis + 1] * spots[first + axis : first + axis + 1, :]
+            t = t + across[:, axis : axis + 1] * spots[first + axis : first + axis + 1, :]
         return t
 
     with jax.named_scope("tables"):
@@ -192,18 +212,22 @@
         lat[0:6, 0:400] = lat_ref[...].astype(F32)
         chosen = (lax.broadcasted_iota(jnp.int32, (512, 1024), 0) == pair).astype(BF16)
         spots = jnp.dot(lat[...].astype(BF16), chosen, preferred_element_type=F32)
-        ang = turn(kp_ref, 0, NKA)
+        ang = turn(kp_ref, 0, None)
         ang = (2.0 * math.pi) * (ang - jnp.round(ang))
         ck[...] = jnp.cos(ang)
         sk[...] = jnp.sin(ang)
-        ang = turn(qp_ref, 3, NPB) + quarter
+        ang = turn(qp_ref, 3, [2 * y + core for core in range(2) for y in range(8)]) + quarter
         ang = (2.0 * math.pi) * (ang - jnp.round(ang))
         cq[...] = jnp.cos(ang)
         sq[...] = jnp.sin(ang)
 
-    real, imag = vectors[0:64], vectors[64:128]
-    near0 = jnp.concatenate([real, imag], axis=1)
-    near1 = jnp.concatenate([-imag, real], axis=1)
+    low32 = low64[0:32]
+    real, imag = vecs[0:32], vecs[32:64]
+    lines[pl.ds(0, 32, stride=2), :] = jnp.where(low32, real, pltpu.roll(imag, 64, 1))
+    lines[pl.ds(1, 32, stride=2), :] = jnp.where(low32, pltpu.roll(real, 64, 1), imag)
+    both = lines[...]
+    near0 = both.astype(BF16)
+    near1 = jnp.where(low64, -pltpu.roll(both, 64, 1), pltpu.roll(both, 64, 1)).astype(BF16)
     wmat[...] = jnp.zeros_like(wmat)
     for i2 in range(2):
         rows0 = pl.ds(i2 * 64, 64)
@@ -218,8 +242,10 @@
     def make_phase(k):
         c = ck[pl.ds(k, 1), :]
         s = sk[pl.ds(k, 1), :]
-        phase[k, 0:16, :] = (c * cq[...] - s * sq[...]).astype(BF16)
-        phase[k, 16:32, :] = (s * cq[...] + c * sq[...]).astype(BF16)
+        for h in range(2):
+            cos_q, sin_q = cq[8 * h : 8 * h + 8, :], sq[8 * h : 8 * h + 8, :]
+            both = jnp.concatenate([c * cos_q - s * sin_q, s * cos_q + c * sin_q], axis=0)
+            phase[h, k] = both.astype(BF16)
 
     with jax.named_scope("phases"):
         loop(0, NKA, make_phase)
@@ -241,18 +267,29 @@
         cols[v, 768:1024] = last.reshape(256, 128)
 
         def part(n):
-            rows = pl.ds(n * 8, 8)
-            got = jnp.dot(
-                phase[rows].reshape(256, 1024), cols[v],
-                preferred_element_type=F32,
-            )
-            bsend[v, rows] = got.astype(BF16).reshape(8, 32, 128)
-
-        with jax.named_scope("bloch"):
-            loop(0, 4, part)
-        with jax.named_scope("bloch_send"):
-            loop(1, NKA, lambda s: b_copy(v, s).start())
-        brecv[v, ka] = bsend[v, ka]
+            h = n // 2
+            side = lax.rem(n + ka // 16, 2)
+            rows = pl.ds(side * 16, 16)
+            with jax.named_scope("bloch"):
+                got = jnp.dot(
+                    phase[h, rows].reshape(256, 1024), cols[v],
+                    preferred_element_type=F32,
+                )
+                bsend[v, h, rows] = got.astype(BF16).reshape(16, 16, 128)
+
+            def send(t):
+                other = side * 16 + lax.rem(ka + t, 16)
+
+                @pl.when(other != ka)
+                def _():
+                    b_copy(v, h, other).start()
+
+            with jax.named_scope("bloch_send"):
+                loop(0, 16, send)
+
+        loop(0, 4, part)
+        brecv[v, 0, ka] = bsend[v, 0, ka]
+        brecv[v, 1, ka] = bsend[v, 1, ka]
 
     loop(0, VS, bloch_of)
 
@@ -260,53 +297,60 @@
         wait_all(table, NX - 1, x_rs)
         wait_all(parts, NPB - 1, p_rs)
 
-    def squares(q):
-        field = jnp.concatenate([tmat[t, pl.ds(q, 32, stride=16), :] for t in range(4)], axis=0)
+    def squares(q, line):
+        field = jnp.concatenate([tmat[t, pl.ds(line, 32, stride=8), :] for t in (0, 2, 1, 3)], axis=0)
         label = jnp.max(parts[q])
         far = table[lax.rem(label, NX), label // NX]
-        turned = field.T.astype(BF16)
+        turned_field = field.T.astype(BF16)
         got = lax.dot_general(
-            turned, jnp.concatenate([far, far], axis=0), (((1,), (1,)), ((), ())),
+            turned_field, jnp.concatenate([far, far], axis=0), (((1,), (1,)), ((), ())),
             preferred_element_type=F32,
         )
         got = got * got
         both = got[0:64] + got[64:128]
         return jnp.where(low, both[0:32], both[32:64]).astype(BF16)
 
-    def rotate(v):
+    def rotate(n):
+        v, h = n // 2, lax.rem(n, 2)
         with jax.named_scope("bloch_wait"):
-            wait_all(brecv.at[v], NKA - 1, b_rs.at[v])
-
-        def near(n):
-            rows = pl.ds(n * 8, 8)
+            wait_all(brecv.at[v, h], NKA - 1, b_rs.at[v, h])
+
+        def near(t):
+            field = brecv[v, h, pl.ds(t * 16, 16)].astype(F32)
             field = jnp.concatenate(
-                [brecv[v, rows, 0:16, :].reshape(128, 128), brecv[v, rows, 16:32, :].reshape(128, 128)],
-                axis=1,
-            )
+                [field[:, 0:8].reshape(128, 128), field[:, 8:16].reshape(128, 128)], axis=1
+            ).astype(BF16)
             got = jnp.dot(field, wmat[...], preferred_element_type=F32)
-            for t in range(4):
-                tmat[t, pl.ds(n * 128, 128), :] = got[:, t * 128 : (t + 1) * 128]
+            for t4 in range(4):
+                tmat[t4, pl.ds(t * 128, 128), :] = got[:, t4 * 128 : (t4 + 1) * 128]
 
         with jax.named_scope("near_rotation"):
-            loop(0, 4, near)
-
-        def four(n):
+            loop(0, 2, near)
+
+        def four(m):
             for s in range(4):
-                q = pb_peer(4 * n + s)
-                qsend[v, q] = squares(q)
+                line = lax.rem(pb // 2 + 4 * m + s, 8)
+                q = 2 * line + h
+                qsend[v, q] = squares(q, line)
 
             def send(s):
-                @pl.when(s > 0)
+                q = 2 * lax.rem(pb // 2 + s, 8) + h
+
+                @pl.when(q != pb)
                 def _():
-                    q_copy(v, s).start()
-
-            loop(4 * n, 4 * n + 4, send)
+                    q_copy(v, q).start()
+
+            loop(4 * m, 4 * m + 4, send)
 
         with jax.named_scope("far_rotation"):
-            loop(0, 4, four)
+            loop(0, 2, four)
+
+    loop(0, 2 * VS, rotate)
+
+    def keep(v):
         qrecv[v, pb] = qsend[v, pb]
 
-    loop(0, VS, rotate)
+    loop(0, VS, keep)
 
     def place(v):
         with jax.named_scope("squares_wait"):
@@ -333,21 +377,28 @@
 
         def drain(v):
             wait_all(csend.at[v], NPB - 1, c_ss.at[v])
-            wait_all(bsend.at[v], NKA - 1, b_ss.at[v])
+            wait_all(bsend.at[v, 0], NKA - 1, b_ss.at[v, 0])
+            wait_all(bsend.at[v, 1], NKA - 1, b_ss.at[v, 1])
             wait_all(qsend.at[v], NPB - 1, q_ss.at[v])
 
         loop(0, VS, drain)
 
 
-def couple(columns, vectors, part, kp, qp, lat):
+def couple(coupling, vectors, part, kp, qp, lat):
     vmem = pl.BlockSpec(memory_space=pltpu.VMEM)
     dma = pltpu.SemaphoreType.DMA
     return pl.pallas_call(
         kernel,
         out_shape=jax.ShapeDtypeStruct((64, 3072), BF16),
-        in_specs=[vmem, vmem, pl.BlockSpec(memory_space=pltpu.SMEM), vmem, vmem, vmem],
+        in_specs=[pl.BlockSpec(memory_space=pl.ANY)] * 6,
         out_specs=vmem,
         scratch_shapes=[
+            pltpu.VMEM((32, 2, 6144), BF16),
+            pltpu.VMEM((1, 8192), BF16),
+            pltpu.VMEM((1, 1), jnp.int32),
+            pltpu.VMEM((3, NKA), F32),
+            pltpu.VMEM((3, NPB), F32),
+            pltpu.VMEM((6, 400), jnp.int32),
             pltpu.VMEM((3072, 128), F32),
             pltpu.VMEM((NPB, 16, 128), F32),
             pltpu.VMEM((VS, NPB, 48, 128), BF16),
@@ -356,41 +407,42 @@
             pltpu.VMEM((VS, 1024, 128), BF16),
             pltpu.VMEM((8, 128), F32),
             pltpu.VMEM((8, 512), F32),
-            pltpu.VMEM((128, 128), F32),
+            pltpu.VMEM((64, 128), F32),
+            pltpu.VMEM((64, 128), F32),
             pltpu.VMEM((64, 128), BF16),
             pltpu.VMEM((8, 128), jnp.int32),
             pltpu.VMEM((NKA, 1024), F32),
             pltpu.VMEM((NKA, 1024), F32),
             pltpu.VMEM((NPB, 1024), F32),
             pltpu.VMEM((NPB, 1024), F32),
-            pltpu.VMEM((NKA, 32, 1024), BF16),
+            pltpu.VMEM((2, NKA, 16, 1024), BF16),
             pltpu.VMEM((256, 512), BF16),
-            pltpu.VMEM((VS, NKA, 32, 128), BF16),
-            pltpu.VMEM((VS, NKA, 32, 128), BF16),
+            pltpu.VMEM((VS, 2, NKA, 16, 128), BF16),
+            pltpu.VMEM((VS, 2, NKA, 16, 128), BF16),
             pltpu.VMEM((NX, NZ, 64, 128), BF16),
             pltpu.VMEM((NPB, 8, 128), jnp.int32),
-            pltpu.VMEM((4, 512, 128), F32),
+            pltpu.VMEM((4, 256, 128), F32),
             pltpu.VMEM((VS, NPB, 32, 128), BF16),
             pltpu.VMEM((VS, NPB, 32, 128), BF16),
             pltpu.VMEM((1536, 128), F32),
             dma((VS,)), dma((VS,)),
             dma(()), dma(()),
-            dma((VS,)), dma((VS,)),
+            dma((VS, 2)), dma((VS, 2)),
             dma((VS,)), dma((VS,)),
             dma(()), dma(()),
             dma(()), dma(()),
             dma(()), dma(()),
+            dma((6,)),
         ],
         compiler_params=pltpu.CompilerParams(
-            collective_id=0, has_side_effects=True, vmem_limit_bytes=40 << 20
+            collective_id=0, has_side_effects=True, vmem_limit_bytes=60 << 20
         ),
         name="couple",
-    )(columns, vectors, part, kp, qp, lat)
+    )(coupling, vectors, part, kp, qp, lat)
 
 
 def body(coupling, eigvecs, partner, kpoints, qpoints, lattice):
-    columns = jnp.pad(coupling.reshape(50, 6144), ((0, 14), (0, 0)))
-    out = couple(columns, eigvecs.reshape(128, 64), partner, kpoints, qpoints, lattice)
+    out = couple(coupling, eigvecs, partner, kpoints, qpoints, lattice)
     return out.reshape(1, 1, 196608)
 
 

time: 60.1 us -> 57.1 us (0.950)
  local copies, waits for them, and re-layouts: 4.1 us -> 2.16 us
  Pallas kernels: 55 us -> 54.1 us
    reshape x2 -> x0, local copies, waits for them, and re-layouts: 2.17 us -> none  [the longest x1 2.09 us: body(): columns = jnp.pad(coupling.reshape(50, 6144), ((0, 14), (0, 0)))]
    reshape x1, local copies, waits for them, and re-layouts: 1.17 us -> 2.16 us  [body(): return out.reshape(1, 1, 196608)]
    pallas_call x1, Pallas kernels: 55 us -> 54.1 us  [couple(): pl.pallas_call(kernel, out_shape=jax.ShapeDtypeStruct((64, 3072), BF16),...]
    unnamed x8 -> x0, local copies, waits for them, and re-layouts: 0.71 us -> none
where the time goes in v4:
time: 57.1 us; the launch traced here: 56.9 us
  Pallas kernels  54.1 us (95%)
  local copies, waits for them, and re-layouts  2.16 us (4%)
  between operations  0.66 us (1%)
    pallas_call x1, Pallas kernels, couple(): pl.pallas_call(kernel, out_shape=jax.ShapeDtypeStruct((64, 3072), BF16),...  54.1 us
    reshape x1, local copies, waits for them, and re-layouts, body(): return out.reshape(1, 1, 196608)  2.16 us

profile of v4, /device:TPU:1, one launch (start us, length us, event | category | flops | bytes accessed | tf_op | source)
XLA Modules:
  0.0 56.9 jit_solution(6658078409577965985)
XLA Ops:
  0.7 54.1 %couple.1 = bf16[64,3072]{1,0:T(8,128)(2,1)} custom-call(bf16[25,2,6144]{2,1,0:T(2,128)(2,1)} %c_hbm.1, bf16[1,8192]{1,0:T(2,128)(2,1)} %vec_hbm.1, s32[1,1]{1,0:T(1,128)S(6)} %copy.7.part_hbm, f32[3,32]{1,0:T(4,128)} %kp_hbm.1, f32[3,16]{1,0:T(4,128)} %qp_hbm.1, s32[6,400]{1,0:T(8,128)} %lat_hbm.1), custom_call_target="tpu_custom_call" | custom-call | tf_op jit(solution)/shard_map/couple/pallas_call | solution.py:390
  54.7 2.2 %reshape.3 = bf16[1,1,196608]{2,1,0:T(2,128)(2,1)} reshape(bf16[64,3072]{1,0:T(8,128)(2,1)} %couple.1) | data formatting | bytes 786432 | tf_op jit(solution)/shard_map/reshape | solution.py:446

commit v5 on v4

--- a/solution.py
+++ b/solution.py
@@ -28,11 +28,35 @@
     zi = ka // NX
     xi = lax.rem(ka, NX)
 
-    def pb_peer(step):
-        return lax.rem(pb + step, NPB)
-
-    def ka_peer(step):
-        return lax.rem(ka + step, NKA)
+    def ring_offset(step, size):
+        side = 1 - 2 * lax.rem(step, 2)
+        return lax.rem(size // 2 + side * ((step + 1) // 2) + size, size)
+
+    core = lax.rem(pb, 2)
+    yi = pb // 2
+    cores = [1 - core, core]
+    xs = [lax.rem(xi + offset, NX) for offset in (2, 1, 3, 0)]
+
+    def pb_each(do):
+        def some(step, carry):
+            y = lax.rem(yi + ring_offset(step, 8), 8)
+            for c in range(2):
+                do(2 * step + c, 2 * y + cores[c])
+            return carry
+
+        lax.fori_loop(0, 7, some, 0)
+        do(14, 2 * yi + cores[0])
+
+    def ka_each(do, first=0, last=NKA - 1):
+        def some(step, carry):
+            z = lax.rem(zi + ring_offset(step, NZ), NZ)
+            for c in range(NX):
+                do(NX * step + c, z * NX + xs[c])
+            return carry
+
+        lax.fori_loop(first // NX, last // NX, some, 0)
+        for c in range(last % NX):
+            do(last - last % NX + c, zi * NX + xs[c])
 
     inputs = [
         pltpu.make_async_copy(c_hbm, c_ref.at[pl.ds(0, 25)], in_sem.at[0]),
@@ -47,27 +71,20 @@
 
     barrier = pltpu.get_barrier_semaphore()
 
-    def greet_pb(step, carry):
-        pl.semaphore_signal(barrier, inc=1, device_id=(pb_peer(step), ka), device_id_type=MESH)
-        return carry
-
-    def greet_ka(step, carry):
-        pl.semaphore_signal(barrier, inc=1, device_id=(pb, ka_peer(step)), device_id_type=MESH)
-        return carry
-
-    lax.fori_loop(1, NPB, greet_pb, 0)
-    lax.fori_loop(1, NKA, greet_ka, 0)
-
-    def c_copy(v, step):
-        to = pb_peer(step)
+    def greet(to):
+        pl.semaphore_signal(barrier, inc=1, device_id=to, device_id_type=MESH)
+
+    pb_each(lambda step, other: greet((other, ka)))
+    ka_each(lambda step, other: greet((pb, other)))
+
+    def c_copy(v, to):
         return pltpu.make_async_remote_copy(
             src_ref=csend.at[v, to], dst_ref=cols.at[v, pl.ds(pl.multiple_of(pb * 48, 16), 48)],
             send_sem=c_ss.at[v], recv_sem=c_rs.at[v],
             device_id=(to, ka), device_id_type=MESH,
         )
 
-    def e_copy(step):
-        to = pb_peer(step)
+    def e_copy(to):
         return pltpu.make_async_remote_copy(
             src_ref=esend.at[to], dst_ref=erecv.at[pb],
             send_sem=e_ss, recv_sem=e_rs,
@@ -90,17 +107,16 @@
             device_id=(pb, zi * NX + other), device_id_type=MESH,
         )
 
-    def p_copy(step):
-        other = pb_peer(step)
+    def p_copy(other):
         return pltpu.make_async_remote_copy(
             src_ref=part, dst_ref=parts.at[pb],
             send_sem=p_ss, recv_sem=p_rs,
             device_id=(other, ka), device_id_type=MESH,
         )
 
-    def b_copy(v, h, other):
-        return pltpu.make_async_remote_copy(
-            src_ref=bsend.at[v, h, other], dst_ref=brecv.at[v, h, ka],
+    def b_copy(v, h, step, other):
+        return pltpu.make_async_remote_copy(
+            src_ref=bsend.at[v, h, step], dst_ref=brecv.at[v, h, ka],
             send_sem=b_ss.at[v, h], recv_sem=b_rs.at[v, h],
             device_id=(pb, other), device_id_type=MESH,
         )
@@ -165,15 +181,15 @@
     with jax.named_scope("entry"):
         pl.semaphore_wait(barrier, NPB - 1 + NKA - 1)
 
-    loop(1, NPB, lambda s: c_copy(0, s).start())
+    pb_each(lambda step, other: c_copy(0, other).start())
     with jax.named_scope("pick"):
         pick(1)
         pick(2)
     esend[...] = rest[...].astype(BF16)
     erecv[pb] = esend[pb]
-    loop(1, NPB, lambda s: e_copy(s).start())
-    loop(1, NPB, lambda s: c_copy(1, s).start())
-    loop(1, NPB, lambda s: c_copy(2, s).start())
+    pb_each(lambda step, other: e_copy(other).start())
+    pb_each(lambda step, other: c_copy(1, other).start())
+    pb_each(lambda step, other: c_copy(2, other).start())
 
     with jax.named_scope("vectors"):
         for copy in inputs[1:]:
@@ -186,7 +202,7 @@
         loop(1, NZ, lambda s: z_copy(s).start())
         part[...] = jnp.broadcast_to(part_ref[...], (8, 128))
         parts[pb] = part[...]
-        loop(1, NPB, lambda s: p_copy(s).start())
+        pb_each(lambda step, other: p_copy(other).start())
 
     def turn(where, first, order):
         points[...] = jnp.zeros_like(points)
@@ -239,16 +255,17 @@
         wmat[rows0, lanes1] = -near1
         wmat[rows1, lanes1] = near0
 
-    def make_phase(k):
+    def make_phase(step, k):
         c = ck[pl.ds(k, 1), :]
         s = sk[pl.ds(k, 1), :]
         for h in range(2):
             cos_q, sin_q = cq[8 * h : 8 * h + 8, :], sq[8 * h : 8 * h + 8, :]
             both = jnp.concatenate([c * cos_q - s * sin_q, s * cos_q + c * sin_q], axis=0)
-            phase[h, k] = both.astype(BF16)
+            phase[h, step] = both.astype(BF16)
 
     with jax.named_scope("phases"):
-        loop(0, NKA, make_phase)
+        ka_each(make_phase)
+        make_phase(NKA - 1, ka)
 
     with jax.named_scope("vectors_wait"):
         wait_all(table.at[0], NZ - 1, z_rs)
@@ -266,30 +283,23 @@
         last = jnp.where(which == v, erecv[...].astype(F32), 0.0).astype(BF16)
         cols[v, 768:1024] = last.reshape(256, 128)
 
-        def part(n):
-            h = n // 2
-            side = lax.rem(n + ka // 16, 2)
-            rows = pl.ds(side * 16, 16)
-            with jax.named_scope("bloch"):
-                got = jnp.dot(
-                    phase[h, rows].reshape(256, 1024), cols[v],
-                    preferred_element_type=F32,
-                )
-                bsend[v, h, rows] = got.astype(BF16).reshape(16, 16, 128)
-
-            def send(t):
-                other = side * 16 + lax.rem(ka + t, 16)
-
-                @pl.when(other != ka)
-                def _():
-                    b_copy(v, h, other).start()
-
-            with jax.named_scope("bloch_send"):
-                loop(0, 16, send)
-
-        loop(0, 4, part)
-        brecv[v, 0, ka] = bsend[v, 0, ka]
-        brecv[v, 1, ka] = bsend[v, 1, ka]
+        for h in range(2):
+            for first in (0, 16):
+                rows = pl.ds(first, 16)
+                with jax.named_scope("bloch"):
+                    got = jnp.dot(
+                        phase[h, rows].reshape(256, 1024), cols[v],
+                        preferred_element_type=F32,
+                    )
+                    bsend[v, h, rows] = got.astype(BF16).reshape(16, 16, 128)
+                with jax.named_scope("bloch_send"):
+                    ka_each(
+                        lambda step, other: b_copy(v, h, step, other).start(),
+                        first, min(first + 16, NKA - 1),
+                    )
+
+        brecv[v, 0, ka] = bsend[v, 0, NKA - 1]
+        brecv[v, 1, ka] = bsend[v, 1, NKA - 1]
 
     loop(0, VS, bloch_of)
 
@@ -328,19 +338,17 @@
             loop(0, 2, near)
 
         def four(m):
+            others = []
             for s in range(4):
-                line = lax.rem(pb // 2 + 4 * m + s, 8)
+                line = lax.rem(yi + ring_offset(4 * m + s, 8), 8)
                 q = 2 * line + h
+                others.append(q)
                 qsend[v, q] = squares(q, line)
 
-            def send(s):
-                q = 2 * lax.rem(pb // 2 + s, 8) + h
-
-                @pl.when(q != pb)
+            for s in range(4):
+                @pl.when(others[s] != pb)
                 def _():
-                    q_copy(v, q).start()
-
-            loop(4 * m, 4 * m + 4, send)
+                    q_copy(v, others[s]).start()
 
         with jax.named_scope("far_rotation"):
             loop(0, 2, four)
@@ -390,7 +398,7 @@
     return pl.pallas_call(
         kernel,
         out_shape=jax.ShapeDtypeStruct((64, 3072), BF16),
-        in_specs=[pl.BlockSpec(memory_space=pl.ANY)] * 6,
+        in_specs=[pl.BlockSpec(memory_space=pltpu.HBM)] * 6,
         out_specs=vmem,
         scratch_shapes=[
             pltpu.VMEM((32, 2, 6144), BF16),

time: 57.1 us -> 55.3 us (0.968)
  Pallas kernels: 54.1 us -> 52.3 us
    pallas_call x1, Pallas kernels: 54.1 us -> 52.3 us  [couple(): pl.pallas_call(kernel, out_shape=jax.ShapeDtypeStruct((64, 3072), BF16),...]
where the time goes in v5:
time: 55.3 us; the launch traced here: 55.2 us
  Pallas kernels  52.3 us (95%)
  local copies, waits for them, and re-layouts  2.16 us (4%)
  between operations  0.66 us (1%)
    pallas_call x1, Pallas kernels, couple(): pl.pallas_call(kernel, out_shape=jax.ShapeDtypeStruct((64, 3072), BF16),...  52.3 us
    reshape x1, local copies, waits for them, and re-layouts, body(): return out.reshape(1, 1, 196608)  2.16 us

profile of v5, /device:TPU:1, one launch (start us, length us, event | category | flops | bytes accessed | tf_op | source)
XLA Modules:
  0.0 55.2 jit_solution(454367910860018559)
XLA Ops:
  0.7 52.3 %couple.1 = bf16[64,3072]{1,0:T(8,128)(2,1)} custom-call(bf16[25,2,6144]{2,1,0:T(2,128)(2,1)} %c_hbm.1, bf16[1,8192]{1,0:T(2,128)(2,1)} %vec_hbm.1, s32[1,1]{1,0:T(1,128)S(6)} %copy.7.part_hbm, f32[3,32]{1,0:T(4,128)} %kp_hbm.1, f32[3,16]{1,0:T(4,128)} %qp_hbm.1, s32[6,400]{1,0:T(8,128)} %lat_hbm.1), custom_call_target="tpu_custom_call" | custom-call | tf_op jit(solution)/shard_map/couple/pallas_call | solution.py:398
  53.0 2.2 %reshape.3 = bf16[1,1,196608]{2,1,0:T(2,128)(2,1)} reshape(bf16[64,3072]{1,0:T(8,128)(2,1)} %couple.1) | data formatting | bytes 786432 | tf_op jit(solution)/shard_map/reshape | solution.py:454

commit v6 on v5

--- a/solution.py
+++ b/solution.py
@@ -19,9 +19,9 @@
 
 def kernel(
     c_hbm, vec_hbm, part_hbm, kp_hbm, qp_hbm, lat_hbm, out_ref,
-    c_ref, vec_ref, part_ref, kp_ref, qp_ref, lat_ref, turned, rest, csend, esend, erecv, cols, points, lat, vecs, lines, eig, part,
+    c_ref, vec_ref, part_ref, kp_ref, qp_ref, lat_ref, turned, rest, csend, esend, erecv, cols, points, grid, lat, vecs, lines, eig, part,
     ck, sk, cq, sq, phase, wmat, bsend, brecv, table, parts, tmat, qsend, qrecv, spread,
-    c_ss, c_rs, e_ss, e_rs, b_ss, b_rs, q_ss, q_rs, z_ss, z_rs, x_ss, x_rs, p_ss, p_rs, in_sem,
+    c_ss, c_rs, e_ss, e_rs, b_ss, b_rs, q_ss, q_rs, z_ss, z_rs, x_ss, x_rs, m_ss, m_rs, p_ss, p_rs, in_sem, c_sem, inside,
 ):
     pb = lax.axis_index("pb")
     ka = lax.axis_index("ka")
@@ -47,24 +47,26 @@
         lax.fori_loop(0, 7, some, 0)
         do(14, 2 * yi + cores[0])
 
-    def ka_each(do, first=0, last=NKA - 1):
-        def some(step, carry):
-            z = lax.rem(zi + ring_offset(step, NZ), NZ)
+    def planes_each(do, first=0, last=NZ):
+        def some(plane, carry):
             for c in range(NX):
-                do(NX * step + c, z * NX + xs[c])
+                do(NX * plane + c, plane * NX + xs[c], True if c < NX - 1 else plane != zi)
             return carry
 
-        lax.fori_loop(first // NX, last // NX, some, 0)
-        for c in range(last % NX):
-            do(last - last % NX + c, zi * NX + xs[c])
-
+        lax.fori_loop(first, last, some, 0)
+
+    def c_piece(n):
+        lanes = pl.ds(n * 1024, 1024)
+        return pltpu.make_async_copy(c_hbm.at[:, :, lanes], c_ref.at[pl.ds(0, 25), :, lanes], c_sem.at[n])
+
+    for n in (0, 3, 1, 4, 2, 5):
+        c_piece(n).start()
     inputs = [
-        pltpu.make_async_copy(c_hbm, c_ref.at[pl.ds(0, 25)], in_sem.at[0]),
-        pltpu.make_async_copy(vec_hbm, vec_ref, in_sem.at[1]),
-        pltpu.make_async_copy(part_hbm, part_ref, in_sem.at[2]),
-        pltpu.make_async_copy(kp_hbm, kp_ref, in_sem.at[3]),
-        pltpu.make_async_copy(qp_hbm, qp_ref, in_sem.at[4]),
-        pltpu.make_async_copy(lat_hbm, lat_ref, in_sem.at[5]),
+        pltpu.make_async_copy(vec_hbm, vec_ref, in_sem.at[0]),
+        pltpu.make_async_copy(part_hbm, part_ref, in_sem.at[1]),
+        pltpu.make_async_copy(kp_hbm, kp_ref, in_sem.at[2]),
+        pltpu.make_async_copy(qp_hbm, qp_ref, in_sem.at[3]),
+        pltpu.make_async_copy(lat_hbm, lat_ref, in_sem.at[4]),
     ]
     for copy in inputs:
         copy.start()
@@ -75,7 +77,15 @@
         pl.semaphore_signal(barrier, inc=1, device_id=to, device_id_type=MESH)
 
     pb_each(lambda step, other: greet((other, ka)))
-    ka_each(lambda step, other: greet((pb, other)))
+    for c in range(NX - 1):
+        greet((pb, zi * NX + xs[c]))
+
+    def greet_above(plane, carry):
+        for c in range(NX):
+            greet((pb, plane * NX + xs[c]))
+        return carry
+
+    lax.fori_loop(zi + 1, NZ, greet_above, 0)
 
     def c_copy(v, to):
         return pltpu.make_async_remote_copy(
@@ -91,21 +101,34 @@
             device_id=(to, ka), device_id_type=MESH,
         )
 
-    def z_copy(step):
-        other = lax.rem(zi + step, NZ)
-        return pltpu.make_async_remote_copy(
-            src_ref=eig, dst_ref=table.at[xi, zi],
+    def z_copy(plane):
+        return pltpu.make_async_remote_copy(
+            src_ref=eig, dst_ref=table.at[core, xi, zi // 2],
             send_sem=z_ss, recv_sem=z_rs,
-            device_id=(pb, other * NX + xi), device_id_type=MESH,
-        )
-
-    def x_copy(step):
-        other = lax.rem(xi + step, NX)
-        return pltpu.make_async_remote_copy(
-            src_ref=table.at[xi], dst_ref=table.at[xi],
+            device_id=(pb, plane * NX + xi), device_id_type=MESH,
+        )
+
+    def x_copy(other):
+        return pltpu.make_async_remote_copy(
+            src_ref=table.at[core, xi], dst_ref=table.at[core, xi],
             send_sem=x_ss, recv_sem=x_rs,
             device_id=(pb, zi * NX + other), device_id_type=MESH,
         )
+
+    def m_copy():
+        return pltpu.make_async_remote_copy(
+            src_ref=table.at[core], dst_ref=table.at[core],
+            send_sem=m_ss, recv_sem=m_rs,
+            device_id=(2 * yi + cores[0], ka), device_id_type=MESH,
+        )
+
+    def b_send(v, h, step, other, remote):
+        if remote is True:
+            b_copy(v, h, step, other).start()
+        else:
+            @pl.when(remote)
+            def _():
+                b_copy(v, h, step, other).start()
 
     def p_copy(other):
         return pltpu.make_async_remote_copy(
@@ -148,6 +171,8 @@
         return lax.dot_general(unit, block, (((1,), (1,)), ((), ())), preferred_element_type=F32)
 
     def turn_some(n):
+        c_piece(n).wait()
+        c_piece(n + 3).wait()
         for t in range(8):
             first = pl.multiple_of((8 * n + t) * 128, 128)
             second = pl.multiple_of(3072 + (8 * n + t) * 128, 128)
@@ -172,16 +197,25 @@
 
     rest[...] = jnp.zeros_like(rest)
     c_ref[25:32] = jnp.zeros((7, 2, 6144), BF16)
-    inputs[0].wait()
     with jax.named_scope("transpose"):
         loop(0, 3, turn_some)
     with jax.named_scope("pick"):
         pick(0)
 
     with jax.named_scope("entry"):
-        pl.semaphore_wait(barrier, NPB - 1 + NKA - 1)
+        pl.semaphore_wait(barrier, NPB - 1 + NX - 1 + NX * zi)
 
     pb_each(lambda step, other: c_copy(0, other).start())
+
+    def tell_below(plane, carry):
+        for c in range(NX):
+            pl.semaphore_signal(
+                inside.at[zi], inc=1, device_id=(pb, plane * NX + xs[c]), device_id_type=MESH
+            )
+        return carry
+
+    lax.fori_loop(0, zi, tell_below, 0)
+
     with jax.named_scope("pick"):
         pick(1)
         pick(2)
@@ -192,14 +226,18 @@
     pb_each(lambda step, other: c_copy(2, other).start())
 
     with jax.named_scope("vectors"):
-        for copy in inputs[1:]:
+        for copy in inputs:
             copy.wait()
         for t in range(64):
             vecs[t : t + 1, :] = vec_ref[:, t * 128 : (t + 1) * 128].astype(F32)
         across = jnp.concatenate([vecs[...], vecs[...]], axis=0).T
         eig[...] = jnp.where(low64, across[0:64], across[64:128]).astype(BF16)
-        table[xi, zi] = eig[...]
-        loop(1, NZ, lambda s: z_copy(s).start())
+
+        @pl.when(lax.rem(zi, 2) == core)
+        def _():
+            table[core, xi, zi // 2] = eig[...]
+            loop(0, zi, lambda plane: z_copy(plane).start())
+
         part[...] = jnp.broadcast_to(part_ref[...], (8, 128))
         parts[pb] = part[...]
         pb_each(lambda step, other: p_copy(other).start())
@@ -211,7 +249,8 @@
         if order is None:
             across = across[0:NKA]
         else:
-            across = jnp.concatenate([across[q : q + 1] for q in order], axis=0)
+            grid[...] = jnp.concatenate([across[0:NPB], jnp.zeros((NPB, 120), F32)], axis=1)
+            across = jnp.concatenate([grid[pl.ds(q, 2), :] for q in order], axis=0)
         t = jnp.zeros((across.shape[0], 1024), F32)
         for axis in range(3):
             t = t + across[:, axis : axis + 1] * spots[first + axis : first + axis + 1, :]
@@ -232,7 +271,7 @@
         ang = (2.0 * math.pi) * (ang - jnp.round(ang))
         ck[...] = jnp.cos(ang)
         sk[...] = jnp.sin(ang)
-        ang = turn(qp_ref, 3, [2 * y + core for core in range(2) for y in range(8)]) + quarter
+        ang = turn(qp_ref, 3, [2 * lax.rem(yi + ring_offset(t, 8), 8) for t in range(8)]) + quarter
         ang = (2.0 * math.pi) * (ang - jnp.round(ang))
         cq[...] = jnp.cos(ang)
         sq[...] = jnp.sin(ang)
@@ -255,7 +294,7 @@
         wmat[rows0, lanes1] = -near1
         wmat[rows1, lanes1] = near0
 
-    def make_phase(step, k):
+    def make_phase(step, k, other):
         c = ck[pl.ds(k, 1), :]
         s = sk[pl.ds(k, 1), :]
         for h in range(2):
@@ -264,12 +303,17 @@
             phase[h, step] = both.astype(BF16)
 
     with jax.named_scope("phases"):
-        ka_each(make_phase)
-        make_phase(NKA - 1, ka)
-
-    with jax.named_scope("vectors_wait"):
-        wait_all(table.at[0], NZ - 1, z_rs)
-        loop(1, NX, lambda s: x_copy(s).start())
+        planes_each(make_phase)
+
+    with jax.named_scope("inside"):
+        def enter_above(plane):
+            pl.semaphore_wait(inside.at[plane], NX)
+
+            @pl.when(lax.rem(zi, 2) == core)
+            def _():
+                z_copy(plane).start()
+
+        loop(zi + 1, NZ, enter_above)
 
     with jax.named_scope("rest_wait"):
         wait_all(erecv, NPB - 1, e_rs)
@@ -293,24 +337,39 @@
                     )
                     bsend[v, h, rows] = got.astype(BF16).reshape(16, 16, 128)
                 with jax.named_scope("bloch_send"):
-                    ka_each(
-                        lambda step, other: b_copy(v, h, step, other).start(),
-                        first, min(first + 16, NKA - 1),
-                    )
-
-        brecv[v, 0, ka] = bsend[v, 0, NKA - 1]
-        brecv[v, 1, ka] = bsend[v, 1, NKA - 1]
-
-    loop(0, VS, bloch_of)
-
-    with jax.named_scope("vectors_wait_x"):
-        wait_all(table, NX - 1, x_rs)
-        wait_all(parts, NPB - 1, p_rs)
+                    planes_each(lambda *peer: b_send(v, h, *peer), first // NX, first // NX + 4)
+
+        brecv[v, 0, ka] = bsend[v, 0, NX * zi + NX - 1]
+        brecv[v, 1, ka] = bsend[v, 1, NX * zi + NX - 1]
+
+    def vectors_x():
+        with jax.named_scope("vectors_wait_z"):
+            @pl.when(lax.rem(zi, 2) == core)
+            def _():
+                wait_all(table.at[0, 0], NZ // 2 - 1, z_rs)
+
+            @pl.when(lax.rem(zi, 2) != core)
+            def _():
+                wait_all(table.at[0, 0], NZ // 2, z_rs)
+
+            for c in range(NX - 1):
+                x_copy(xs[c]).start()
+
+    def vectors_core():
+        with jax.named_scope("vectors_wait_x"):
+            wait_all(table.at[0], NX - 1, x_rs)
+            m_copy().start()
+
+    def vectors_done():
+        with jax.named_scope("vectors_wait"):
+            wait_all(table, 1, m_rs)
+            wait_all(parts, NPB - 1, p_rs)
 
     def squares(q, line):
         field = jnp.concatenate([tmat[t, pl.ds(line, 32, stride=8), :] for t in (0, 2, 1, 3)], axis=0)
         label = jnp.max(parts[q])
-        far = table[lax.rem(label, NX), label // NX]
+        plane = label // NX
+        far = table[lax.rem(plane, 2), lax.rem(label, NX), plane // 2]
         turned_field = field.T.astype(BF16)
         got = lax.dot_general(
             turned_field, jnp.concatenate([far, far], axis=0), (((1,), (1,)), ((), ())),
@@ -340,8 +399,8 @@
         def four(m):
             others = []
             for s in range(4):
-                line = lax.rem(yi + ring_offset(4 * m + s, 8), 8)
-                q = 2 * line + h
+                line = 4 * m + s
+                q = 2 * lax.rem(yi + ring_offset(4 * h + 2 * m + s // 2, 8), 8) + s % 2
                 others.append(q)
                 qsend[v, q] = squares(q, line)
 
@@ -353,6 +412,21 @@
         with jax.named_scope("far_rotation"):
             loop(0, 2, four)
 
+    @pl.when(zi >= 3)
+    def _():
+        vectors_x()
+
+    bloch_of(0)
+
+    @pl.when(zi < 3)
+    def _():
+        vectors_x()
+
+    bloch_of(1)
+    vectors_core()
+
+    bloch_of(2)
+    vectors_done()
     loop(0, 2 * VS, rotate)
 
     def keep(v):
@@ -378,8 +452,13 @@
             out_ref[:, 1536 + n * 128 : 1536 + (n + 1) * 128] = block[64:128]
 
     with jax.named_scope("drain"):
-        wait_all(table.at[0], NZ - 1, z_ss)
-        wait_all(table, NX - 1, x_ss)
+        @pl.when(lax.rem(zi, 2) == core)
+        def _():
+            gone = cols.at[0, pl.ds(0, 64 * (NZ - 1))]
+            pltpu.make_async_copy(gone, gone, z_ss).wait()
+
+        wait_all(table.at[0], NX - 1, x_ss)
+        wait_all(table, 1, m_ss)
         wait_all(parts, NPB - 1, p_ss)
         wait_all(esend, NPB - 1, e_ss)
 
@@ -414,6 +493,7 @@
             pltpu.VMEM((NPB, 16, 128), BF16),
             pltpu.VMEM((VS, 1024, 128), BF16),
             pltpu.VMEM((8, 128), F32),
+            pltpu.VMEM((NPB, 128), F32),
             pltpu.VMEM((8, 512), F32),
             pltpu.VMEM((64, 128), F32),
             pltpu.VMEM((64, 128), F32),
@@ -427,7 +507,7 @@
             pltpu.VMEM((256, 512), BF16),
             pltpu.VMEM((VS, 2, NKA, 16, 128), BF16),
             pltpu.VMEM((VS, 2, NKA, 16, 128), BF16),
-            pltpu.VMEM((NX, NZ, 64, 128), BF16),
+            pltpu.VMEM((2, NX, NZ // 2, 64, 128), BF16),
             pltpu.VMEM((NPB, 8, 128), jnp.int32),
             pltpu.VMEM((4, 256, 128), F32),
             pltpu.VMEM((VS, NPB, 32, 128), BF16),
@@ -440,7 +520,10 @@
             dma(()), dma(()),
             dma(()), dma(()),
             dma(()), dma(()),
+            dma(()), dma(()),
+            dma((5,)),
             dma((6,)),
+            pltpu.SemaphoreType.REGULAR((NZ,)),
         ],
         compiler_params=pltpu.CompilerParams(
             collective_id=0, has_side_effects=True, vmem_limit_bytes=60 << 20

time: 55.3 us -> 53.7 us (0.971)
  Pallas kernels: 52.3 us -> 50.7 us
    pallas_call x1, Pallas kernels: 52.3 us -> 50.7 us  [couple(): pl.pallas_call(kernel, out_shape=jax.ShapeDtypeStruct((64, 3072), BF16),...]
where the time goes in v6:
time: 53.7 us; the launch traced here: 53.6 us
  Pallas kernels  50.7 us (94%)
  local copies, waits for them, and re-layouts  2.16 us (4%)
  between operations  0.66 us (1%)
    pallas_call x1, Pallas kernels, couple(): pl.pallas_call(kernel, out_shape=jax.ShapeDtypeStruct((64, 3072), BF16),...  50.7 us
    reshape x1, local copies, waits for them, and re-layouts, body(): return out.reshape(1, 1, 196608)  2.16 us

profile of v6, /device:TPU:1, one launch (start us, length us, event | category | flops | bytes accessed | tf_op | source)
XLA Modules:
  0.0 53.6 jit_solution(7608541545472246011)
XLA Ops:
  0.7 50.7 %couple.1 = bf16[64,3072]{1,0:T(8,128)(2,1)} custom-call(bf16[25,2,6144]{2,1,0:T(2,128)(2,1)} %c_hbm.1, bf16[1,8192]{1,0:T(2,128)(2,1)} %vec_hbm.1, s32[1,1]{1,0:T(1,128)S(6)} %copy.7.part_hbm, f32[3,32]{1,0:T(4,128)} %kp_hbm.1, f32[3,16]{1,0:T(4,128)} %qp_hbm.1, s32[6,400]{1,0:T(8,128)} %lat_hbm.1), custom_call_target="tpu_custom_call" | custom-call | tf_op jit(solution)/shard_map/couple/pallas_call | solution.py:477
  51.4 2.2 %reshape.3 = bf16[1,1,196608]{2,1,0:T(2,128)(2,1)} reshape(bf16[64,3072]{1,0:T(8,128)(2,1)} %couple.1) | data formatting | bytes 786432 | tf_op jit(solution)/shard_map/reshape | solution.py:537

commit v7 on v6

--- a/solution.py
+++ b/solution.py
@@ -19,9 +19,9 @@
 
 def kernel(
     c_hbm, vec_hbm, part_hbm, kp_hbm, qp_hbm, lat_hbm, out_ref,
-    c_ref, vec_ref, part_ref, kp_ref, qp_ref, lat_ref, turned, rest, csend, esend, erecv, cols, points, grid, lat, vecs, lines, eig, part,
+    c_ref, vec_ref, part_ref, kp_ref, qp_ref, lat_ref, turned, csend, crecv, cols, points, grid, lat, vecs, lines, eig, part,
     ck, sk, cq, sq, phase, wmat, bsend, brecv, table, parts, tmat, qsend, qrecv, spread,
-    c_ss, c_rs, e_ss, e_rs, b_ss, b_rs, q_ss, q_rs, z_ss, z_rs, x_ss, x_rs, m_ss, m_rs, p_ss, p_rs, in_sem, c_sem, inside,
+    c_ss, c_rs, b_ss, b_rs, q_ss, q_rs, z_ss, z_rs, x_ss, x_rs, m_ss, m_rs, p_ss, p_rs, in_sem, c_sem, inside,
 ):
     pb = lax.axis_index("pb")
     ka = lax.axis_index("ka")
@@ -89,15 +89,8 @@
 
     def c_copy(v, to):
         return pltpu.make_async_remote_copy(
-            src_ref=csend.at[v, to], dst_ref=cols.at[v, pl.ds(pl.multiple_of(pb * 48, 16), 48)],
+            src_ref=csend.at[v, to], dst_ref=crecv.at[v, pb],
             send_sem=c_ss.at[v], recv_sem=c_rs.at[v],
-            device_id=(to, ka), device_id_type=MESH,
-        )
-
-    def e_copy(to):
-        return pltpu.make_async_remote_copy(
-            src_ref=esend.at[to], dst_ref=erecv.at[pb],
-            send_sem=e_ss, recv_sem=e_rs,
             device_id=(to, ka), device_id_type=MESH,
         )
 
@@ -189,13 +182,11 @@
                 field = turned[pl.ds(3 * to + v, 64, stride=48), :].astype(BF16)
                 got = flip(jnp.concatenate([field, field], axis=0))
                 got = jnp.where(low64, got[0:64], got[64:128])
-                csend[v, to] = got[0:48].astype(BF16)
-                rest[to, 2 * v : 2 * v + 2, :] = got[48:50]
+                csend[v, to] = got[0:50].astype(BF16).reshape(25, 2, 128)
 
         loop(0, 2, some)
-        cols[v, pl.ds(pl.multiple_of(pb * 48, 16), 48)] = csend[v, pb]
-
-    rest[...] = jnp.zeros_like(rest)
+        crecv[v, pb] = csend[v, pb]
+
     c_ref[25:32] = jnp.zeros((7, 2, 6144), BF16)
     with jax.named_scope("transpose"):
         loop(0, 3, turn_some)
@@ -219,9 +210,6 @@
     with jax.named_scope("pick"):
         pick(1)
         pick(2)
-    esend[...] = rest[...].astype(BF16)
-    erecv[pb] = esend[pb]
-    pb_each(lambda step, other: e_copy(other).start())
     pb_each(lambda step, other: c_copy(1, other).start())
     pb_each(lambda step, other: c_copy(2, other).start())
 
@@ -258,10 +246,7 @@
 
     with jax.named_scope("tables"):
         lane = lax.broadcasted_iota(jnp.int32, (1, 1024), 1)
-        source = lax.shift_right_logical(lane * 1366, 16)
-        pair = lax.shift_right_logical(lane - 48 * source, 1)
-        extra = 25 * lax.shift_right_logical(lane - 768, 4) + 24
-        pair = jnp.where(lane < 768, 25 * source + pair, extra)
+        pair = lax.shift_right_logical(lane, 1)
         quarter = jnp.where(lax.bitwise_and(lane, 1) == 1, 0.25, 0.0)
         lat[...] = jnp.zeros_like(lat)
         lat[0:6, 0:400] = lat_ref[...].astype(F32)
@@ -315,24 +300,19 @@
 
         loop(zi + 1, NZ, enter_above)
 
-    with jax.named_scope("rest_wait"):
-        wait_all(erecv, NPB - 1, e_rs)
-
-    which = lax.shift_right_logical(lax.broadcasted_iota(jnp.int32, (NPB, 16, 128), 1), 1)
+    cols[800:1024] = jnp.zeros((224, 128), BF16)
 
     def bloch_of(v):
         with jax.named_scope("couplings_wait"):
-            arrived = cols.at[v, pl.ds(0, 48 * (NPB - 1))]
-            pltpu.make_async_copy(arrived, arrived, c_rs.at[v]).wait()
-        last = jnp.where(which == v, erecv[...].astype(F32), 0.0).astype(BF16)
-        cols[v, 768:1024] = last.reshape(256, 128)
+            wait_all(crecv.at[v], NPB - 1, c_rs.at[v])
+            cols[0:800] = crecv[v].reshape(800, 128)
 
         for h in range(2):
             for first in (0, 16):
                 rows = pl.ds(first, 16)
                 with jax.named_scope("bloch"):
                     got = jnp.dot(
-                        phase[h, rows].reshape(256, 1024), cols[v],
+                        phase[h, rows].reshape(256, 1024), cols[...],
                         preferred_element_type=F32,
                     )
                     bsend[v, h, rows] = got.astype(BF16).reshape(16, 16, 128)
@@ -454,13 +434,12 @@
     with jax.named_scope("drain"):
         @pl.when(lax.rem(zi, 2) == core)
         def _():
-            gone = cols.at[0, pl.ds(0, 64 * (NZ - 1))]
+            gone = cols.at[pl.ds(0, 64 * (NZ - 1))]
             pltpu.make_async_copy(gone, gone, z_ss).wait()
 
         wait_all(table.at[0], NX - 1, x_ss)
         wait_all(table, 1, m_ss)
         wait_all(parts, NPB - 1, p_ss)
-        wait_all(esend, NPB - 1, e_ss)
 
         def drain(v):
             wait_all(csend.at[v], NPB - 1, c_ss.at[v])
@@ -487,11 +466,9 @@
             pltpu.VMEM((3, NPB), F32),
             pltpu.VMEM((6, 400), jnp.int32),
             pltpu.VMEM((3072, 128), F32),
-            pltpu.VMEM((NPB, 16, 128), F32),
-            pltpu.VMEM((VS, NPB, 48, 128), BF16),
-            pltpu.VMEM((NPB, 16, 128), BF16),
-            pltpu.VMEM((NPB, 16, 128), BF16),
-            pltpu.VMEM((VS, 1024, 128), BF16),
+            pltpu.VMEM((VS, NPB, 25, 2, 128), BF16),
+            pltpu.VMEM((VS, NPB, 25, 2, 128), BF16),
+            pltpu.VMEM((1024, 128), BF16),
             pltpu.VMEM((8, 128), F32),
             pltpu.VMEM((NPB, 128), F32),
             pltpu.VMEM((8, 512), F32),
@@ -514,7 +491,6 @@
             pltpu.VMEM((VS, NPB, 32, 128), BF16),
             pltpu.VMEM((1536, 128), F32),
             dma((VS,)), dma((VS,)),
-            dma(()), dma(()),
             dma((VS, 2)), dma((VS, 2)),
             dma((VS,)), dma((VS,)),
             dma(()), dma(()),

time: 53.7 us -> 51.9 us (0.966)
  Pallas kernels: 50.7 us -> 48.9 us
    pallas_call x1, Pallas kernels: 50.7 us -> 48.9 us  [couple(): pl.pallas_call(kernel, out_shape=jax.ShapeDtypeStruct((64, 3072), BF16),...]
where the time goes in v7:
time: 51.9 us; the launch traced here: 51.7 us
  Pallas kernels  48.9 us (94%)
  local copies, waits for them, and re-layouts  2.16 us (4%)
  between operations  0.66 us (1%)
    pallas_call x1, Pallas kernels, couple(): pl.pallas_call(kernel, out_shape=jax.ShapeDtypeStruct((64, 3072), BF16),...  48.9 us
    reshape x1, local copies, waits for them, and re-layouts, body(): return out.reshape(1, 1, 196608)  2.16 us

profile of v7, /device:TPU:1, one launch (start us, length us, event | category | flops | bytes accessed | tf_op | source)
XLA Modules:
  0.0 51.7 jit_solution(16306296211640689866)
XLA Ops:
  0.7 48.9 %couple.1 = bf16[64,3072]{1,0:T(8,128)(2,1)} custom-call(bf16[25,2,6144]{2,1,0:T(2,128)(2,1)} %c_hbm.1, bf16[1,8192]{1,0:T(2,128)(2,1)} %vec_hbm.1, s32[1,1]{1,0:T(1,128)S(6)} %copy.7.part_hbm, f32[3,32]{1,0:T(4,128)} %kp_hbm.1, f32[3,16]{1,0:T(4,128)} %qp_hbm.1, s32[6,400]{1,0:T(8,128)} %lat_hbm.1), custom_call_target="tpu_custom_call" | custom-call | tf_op jit(solution)/shard_map/couple/pallas_call | solution.py:456
  49.5 2.2 %reshape.3 = bf16[1,1,196608]{2,1,0:T(2,128)(2,1)} reshape(bf16[64,3072]{1,0:T(8,128)(2,1)} %couple.1) | data formatting | bytes 786432 | tf_op jit(solution)/shard_map/reshape | solution.py:513

commit v8 on v7

--- a/solution.py
+++ b/solution.py
@@ -19,9 +19,9 @@
 
 def kernel(
     c_hbm, vec_hbm, part_hbm, kp_hbm, qp_hbm, lat_hbm, out_ref,
-    c_ref, vec_ref, part_ref, kp_ref, qp_ref, lat_ref, turned, csend, crecv, cols, points, grid, lat, vecs, lines, eig, part,
-    ck, sk, cq, sq, phase, wmat, bsend, brecv, table, parts, tmat, qsend, qrecv, spread,
-    c_ss, c_rs, b_ss, b_rs, q_ss, q_rs, z_ss, z_rs, x_ss, x_rs, m_ss, m_rs, p_ss, p_rs, in_sem, c_sem, inside,
+    c_ref, vec_ref, part_ref, kp_ref, qp_ref, lat_ref, turned, asend, arecv, csend, crecv, cols, acols, points, grid, lat, vecs, lines, eig, part,
+    ck, sk, cq, sq, phase, wmat, wfold, bsend, brecv, table, parts, tmat, qsend, qrecv, spread,
+    a_ss, a_rs, c_ss, c_rs, b_ss, b_rs, q_ss, q_rs, z_ss, z_rs, x_ss, x_rs, m_ss, m_rs, p_ss, p_rs, in_sem, c_sem, inside,
 ):
     pb = lax.axis_index("pb")
     ka = lax.axis_index("ka")
@@ -87,10 +87,17 @@
 
     lax.fori_loop(zi + 1, NZ, greet_above, 0)
 
+    def a_copy(i2, to):
+        return pltpu.make_async_remote_copy(
+            src_ref=asend.at[i2, to], dst_ref=arecv.at[i2, pb],
+            send_sem=a_ss.at[i2], recv_sem=a_rs.at[i2],
+            device_id=(to, ka), device_id_type=MESH,
+        )
+
     def c_copy(v, to):
         return pltpu.make_async_remote_copy(
-            src_ref=csend.at[v, to], dst_ref=crecv.at[v, pb],
-            send_sem=c_ss.at[v], recv_sem=c_rs.at[v],
+            src_ref=csend.at[v - 1, to], dst_ref=crecv.at[v - 1, pb],
+            send_sem=c_ss.at[v - 1], recv_sem=c_rs.at[v - 1],
             device_id=(to, ka), device_id_type=MESH,
         )
 
@@ -160,8 +167,12 @@
     line = lax.broadcasted_iota(jnp.int32, (128, 128), 0)
     unit = (line == lax.broadcasted_iota(jnp.int32, (128, 128), 1)).astype(BF16)
 
-    def flip(block):
-        return lax.dot_general(unit, block, (((1,), (1,)), ((), ())), preferred_element_type=F32)
+    inner = lax.bitwise_and(line, 63)
+    moved = (line - inner) + 2 * lax.bitwise_and(inner, 31) + lax.shift_right_logical(inner, 5)
+    by_part = (moved == lax.broadcasted_iota(jnp.int32, (128, 128), 1)).astype(BF16)
+
+    def flip(block, order=unit):
+        return lax.dot_general(order, block, (((1,), (1,)), ((), ())), preferred_element_type=F32)
 
     def turn_some(n):
         c_piece(n).wait()
@@ -175,28 +186,41 @@
             )
             turned[pl.ds(first, 128), :] = flip(both)
 
+    def mode_of(to, v):
+        field = turned[pl.ds(3 * to + v, 64, stride=48), :].astype(BF16)
+        return jnp.concatenate([field, field], axis=0)
+
+    def pick_folded(n):
+        for t in range(8):
+            to = 8 * n + t
+            got = flip(mode_of(to, 0), by_part)
+            for i2 in range(2):
+                block = jnp.where(low, got[64 * i2 : 64 * i2 + 32], got[64 * i2 + 32 : 64 * i2 + 64])
+                asend[i2, to] = block[0:26].astype(BF16).reshape(13, 2, 128)
+
     def pick(v):
         def some(n):
             for t in range(8):
                 to = 8 * n + t
-                field = turned[pl.ds(3 * to + v, 64, stride=48), :].astype(BF16)
-                got = flip(jnp.concatenate([field, field], axis=0))
+                got = flip(mode_of(to, v))
                 got = jnp.where(low64, got[0:64], got[64:128])
-                csend[v, to] = got[0:50].astype(BF16).reshape(25, 2, 128)
+                csend[v - 1, to] = got[0:50].astype(BF16).reshape(25, 2, 128)
 
         loop(0, 2, some)
-        crecv[v, pb] = csend[v, pb]
+        crecv[v - 1, pb] = csend[v - 1, pb]
 
     c_ref[25:32] = jnp.zeros((7, 2, 6144), BF16)
     with jax.named_scope("transpose"):
         loop(0, 3, turn_some)
     with jax.named_scope("pick"):
-        pick(0)
+        loop(0, 2, pick_folded)
+        arecv[:, pb] = asend[:, pb]
 
     with jax.named_scope("entry"):
         pl.semaphore_wait(barrier, NPB - 1 + NX - 1 + NX * zi)
 
-    pb_each(lambda step, other: c_copy(0, other).start())
+    pb_each(lambda step, other: a_copy(0, other).start())
+    pb_each(lambda step, other: a_copy(1, other).start())
 
     def tell_below(plane, carry):
         for c in range(NX):
@@ -239,18 +263,21 @@
         else:
             grid[...] = jnp.concatenate([across[0:NPB], jnp.zeros((NPB, 120), F32)], axis=1)
             across = jnp.concatenate([grid[pl.ds(q, 2), :] for q in order], axis=0)
-        t = jnp.zeros((across.shape[0], 1024), F32)
+        t = jnp.zeros((across.shape[0], 2048), F32)
         for axis in range(3):
             t = t + across[:, axis : axis + 1] * spots[first + axis : first + axis + 1, :]
         return t
 
     with jax.named_scope("tables"):
-        lane = lax.broadcasted_iota(jnp.int32, (1, 1024), 1)
-        pair = lax.shift_right_logical(lane, 1)
-        quarter = jnp.where(lax.bitwise_and(lane, 1) == 1, 0.25, 0.0)
+        lane = lax.broadcasted_iota(jnp.int32, (1, 2048), 1)
+        inner = lax.bitwise_and(lane, 511)
+        folded = inner - lax.shift_right_logical(inner * 2521, 16)
+        pair = jnp.where(lane < 1024, lax.shift_right_logical(lane, 1), folded)
+        second = jnp.where(lane < 1024, lax.bitwise_and(lane, 1), lax.shift_right_logical(lane - 1024, 9))
+        quarter = jnp.where(second == 1, 0.25, 0.0)
         lat[...] = jnp.zeros_like(lat)
         lat[0:6, 0:400] = lat_ref[...].astype(F32)
-        chosen = (lax.broadcasted_iota(jnp.int32, (512, 1024), 0) == pair).astype(BF16)
+        chosen = (lax.broadcasted_iota(jnp.int32, (512, 2048), 0) == pair).astype(BF16)
         spots = jnp.dot(lat[...].astype(BF16), chosen, preferred_element_type=F32)
         ang = turn(kp_ref, 0, None)
         ang = (2.0 * math.pi) * (ang - jnp.round(ang))
@@ -269,6 +296,7 @@
     near0 = both.astype(BF16)
     near1 = jnp.where(low64, -pltpu.roll(both, 64, 1), pltpu.roll(both, 64, 1)).astype(BF16)
     wmat[...] = jnp.zeros_like(wmat)
+    wfold[...] = jnp.zeros_like(wfold)
     for i2 in range(2):
         rows0 = pl.ds(i2 * 64, 64)
         rows1 = pl.ds(128 + i2 * 64, 64)
@@ -278,6 +306,12 @@
         wmat[rows1, lanes0] = near1
         wmat[rows0, lanes1] = -near1
         wmat[rows1, lanes1] = near0
+        rows0 = pl.ds(i2 * 128, 64)
+        rows1 = pl.ds(i2 * 128 + 64, 64)
+        wfold[rows0, lanes0] = near0
+        wfold[rows1, lanes0] = near1
+        wfold[rows0, lanes1] = -near1
+        wfold[rows1, lanes1] = near0
 
     def make_phase(step, k, other):
         c = ck[pl.ds(k, 1), :]
@@ -301,18 +335,50 @@
         loop(zi + 1, NZ, enter_above)
 
     cols[800:1024] = jnp.zeros((224, 128), BF16)
+    acols[416:512] = jnp.zeros((96, 128), BF16)
+
+    def bloch_folded(i2):
+        with jax.named_scope("couplings_wait"):
+            wait_all(arecv.at[i2], NPB - 1, a_rs.at[i2])
+            acols[0:416] = arecv[i2].reshape(416, 128)
+
+        def part(n):
+            rows = pl.ds(8 * n, 8)
+            with jax.named_scope("bloch"):
+                first = jnp.dot(
+                    phase[:, rows, :, 1024:1536].reshape(256, 512), acols[...], preferred_element_type=F32
+                ).reshape(2, 8, 2, 8, 128)
+                second = jnp.dot(
+                    phase[:, rows, :, 1536:2048].reshape(256, 512), acols[...], preferred_element_type=F32
+                ).reshape(2, 8, 2, 8, 128)
+
+                def across(block):
+                    return pltpu.roll(block.reshape(128, 128), 64, 1).reshape(2, 8, 8, 128)
+
+                real = first[:, :, 0] + across(second[:, :, 0])
+                imag = across(first[:, :, 1]) + second[:, :, 1]
+                both = jnp.where(low_lane, real, imag)
+                both = jnp.concatenate([both[0], both[1]], axis=1)
+                bsend[0, i2, rows] = both.astype(BF16)
+            with jax.named_scope("bloch_send"):
+                planes_each(lambda *peer: b_send(0, i2, *peer), 2 * n, 2 * n + 2)
+
+        loop(0, 4, part)
+        brecv[0, i2, ka] = bsend[0, i2, NX * zi + NX - 1]
+
+    low_lane = lax.broadcasted_iota(jnp.int32, (2, 8, 8, 128), 3) < 64
 
     def bloch_of(v):
         with jax.named_scope("couplings_wait"):
-            wait_all(crecv.at[v], NPB - 1, c_rs.at[v])
-            cols[0:800] = crecv[v].reshape(800, 128)
+            wait_all(crecv.at[v - 1], NPB - 1, c_rs.at[v - 1])
+            cols[0:800] = crecv[v - 1].reshape(800, 128)
 
         for h in range(2):
             for first in (0, 16):
                 rows = pl.ds(first, 16)
                 with jax.named_scope("bloch"):
                     got = jnp.dot(
-                        phase[h, rows].reshape(256, 1024), cols[...],
+                        phase[h, rows, :, 0:1024].reshape(256, 1024), cols[...],
                         preferred_element_type=F32,
                     )
                     bsend[v, h, rows] = got.astype(BF16).reshape(16, 16, 128)
@@ -362,19 +428,37 @@
     def rotate(n):
         v, h = n // 2, lax.rem(n, 2)
         with jax.named_scope("bloch_wait"):
-            wait_all(brecv.at[v, h], NKA - 1, b_rs.at[v, h])
-
-        def near(t):
-            field = brecv[v, h, pl.ds(t * 16, 16)].astype(F32)
-            field = jnp.concatenate(
-                [field[:, 0:8].reshape(128, 128), field[:, 8:16].reshape(128, 128)], axis=1
-            ).astype(BF16)
-            got = jnp.dot(field, wmat[...], preferred_element_type=F32)
+            @pl.when(n == 0)
+            def _():
+                wait_all(brecv.at[0, 0], NKA - 1, b_rs.at[0, 0])
+                wait_all(brecv.at[0, 1], NKA - 1, b_rs.at[0, 1])
+
+            @pl.when(n > 1)
+            def _():
+                wait_all(brecv.at[v, h], NKA - 1, b_rs.at[v, h])
+
+        def near(t, pieces, weights):
+            field = jnp.concatenate([piece.reshape(128, 128) for piece in pieces], axis=1).astype(BF16)
+            got = jnp.dot(field, weights[...], preferred_element_type=F32)
             for t4 in range(4):
                 tmat[t4, pl.ds(t * 128, 128), :] = got[:, t4 * 128 : (t4 + 1) * 128]
 
+        def near_folded(t):
+            fields = [brecv[0, i2, pl.ds(t * 16, 16)].astype(F32) for i2 in range(2)]
+            near(t, [jnp.where(h == 0, field[:, 0:8], field[:, 8:16]) for field in fields], wfold)
+
+        def near_other(t):
+            field = brecv[v, h, pl.ds(t * 16, 16)].astype(F32)
+            near(t, [field[:, 0:8], field[:, 8:16]], wmat)
+
         with jax.named_scope("near_rotation"):
-            loop(0, 2, near)
+            @pl.when(n < 2)
+            def _():
+                loop(0, 2, near_folded)
+
+            @pl.when(n > 1)
+            def _():
+                loop(0, 2, near_other)
 
         def four(m):
             others = []
@@ -392,11 +476,13 @@
         with jax.named_scope("far_rotation"):
             loop(0, 2, four)
 
+    bloch_folded(0)
+
     @pl.when(zi >= 3)
     def _():
         vectors_x()
 
-    bloch_of(0)
+    bloch_folded(1)
 
     @pl.when(zi < 3)
     def _():
@@ -442,12 +528,14 @@
         wait_all(parts, NPB - 1, p_ss)
 
         def drain(v):
-            wait_all(csend.at[v], NPB - 1, c_ss.at[v])
             wait_all(bsend.at[v, 0], NKA - 1, b_ss.at[v, 0])
             wait_all(bsend.at[v, 1], NKA - 1, b_ss.at[v, 1])
             wait_all(qsend.at[v], NPB - 1, q_ss.at[v])
 
         loop(0, VS, drain)
+        for n in range(2):
+            wait_all(asend.at[n], NPB - 1, a_ss.at[n])
+            wait_all(csend.at[n], NPB - 1, c_ss.at[n])
 
 
 def couple(coupling, vectors, part, kp, qp, lat):
@@ -466,9 +554,12 @@
             pltpu.VMEM((3, NPB), F32),
             pltpu.VMEM((6, 400), jnp.int32),
             pltpu.VMEM((3072, 128), F32),
-            pltpu.VMEM((VS, NPB, 25, 2, 128), BF16),
-            pltpu.VMEM((VS, NPB, 25, 2, 128), BF16),
+            pltpu.VMEM((2, NPB, 13, 2, 128), BF16),
+            pltpu.VMEM((2, NPB, 13, 2, 128), BF16),
+            pltpu.VMEM((VS - 1, NPB, 25, 2, 128), BF16),
+            pltpu.VMEM((VS - 1, NPB, 25, 2, 128), BF16),
             pltpu.VMEM((1024, 128), BF16),
+            pltpu.VMEM((512, 128), BF16),
             pltpu.VMEM((8, 128), F32),
             pltpu.VMEM((NPB, 128), F32),
             pltpu.VMEM((8, 512), F32),
@@ -476,11 +567,12 @@
             pltpu.VMEM((64, 128), F32),
             pltpu.VMEM((64, 128), BF16),
             pltpu.VMEM((8, 128), jnp.int32),
-            pltpu.VMEM((NKA, 1024), F32),
-            pltpu.VMEM((NKA, 1024), F32),
-            pltpu.VMEM((NPB, 1024), F32),
-            pltpu.VMEM((NPB, 1024), F32),
-            pltpu.VMEM((2, NKA, 16, 1024), BF16),
+            pltpu.VMEM((NKA, 2048), F32),
+            pltpu.VMEM((NKA, 2048), F32),
+            pltpu.VMEM((NPB, 2048), F32),
+            pltpu.VMEM((NPB, 2048), F32),
+            pltpu.VMEM((2, NKA, 16, 2048), BF16),
+            pltpu.VMEM((256, 512), BF16),
             pltpu.VMEM((256, 512), BF16),
             pltpu.VMEM((VS, 2, NKA, 16, 128), BF16),
             pltpu.VMEM((VS, 2, NKA, 16, 128), BF16),
@@ -490,7 +582,8 @@
             pltpu.VMEM((VS, NPB, 32, 128), BF16),
             pltpu.VMEM((VS, NPB, 32, 128), BF16),
             pltpu.VMEM((1536, 128), F32),
-            dma((VS,)), dma((VS,)),
+            dma((2,)), dma((2,)),
+            dma((VS - 1,)), dma((VS - 1,)),
             dma((VS, 2)), dma((VS, 2)),
             dma((VS,)), dma((VS,)),
             dma(()), dma(()),

time: 51.9 us -> 50.7 us (0.977)
  Pallas kernels: 48.9 us -> 47.7 us
    pallas_call x1, Pallas kernels: 48.9 us -> 47.7 us  [couple(): pl.pallas_call(kernel, out_shape=jax.ShapeDtypeStruct((64, 3072), BF16),...]
where the time goes in v8:
time: 50.7 us; the launch traced here: 50.5 us
  Pallas kernels  47.7 us (94%)
  local copies, waits for them, and re-layouts  2.16 us (4%)
  between operations  0.66 us (1%)
    pallas_call x1, Pallas kernels, couple(): pl.pallas_call(kernel, out_shape=jax.ShapeDtypeStruct((64, 3072), BF16),...  47.7 us
    reshape x1, local copies, waits for them, and re-layouts, body(): return out.reshape(1, 1, 196608)  2.16 us

profile of v8, /device:TPU:1, one launch (start us, length us, event | category | flops | bytes accessed | tf_op | source)
XLA Modules:
  0.0 50.5 jit_solution(3290809022123551392)
XLA Ops:
  0.7 47.7 %couple.1 = bf16[64,3072]{1,0:T(8,128)(2,1)} custom-call(bf16[25,2,6144]{2,1,0:T(2,128)(2,1)} %c_hbm.1, bf16[1,8192]{1,0:T(2,128)(2,1)} %vec_hbm.1, s32[1,1]{1,0:T(1,128)S(6)} %copy.7.part_hbm, f32[3,32]{1,0:T(4,128)} %kp_hbm.1, f32[3,16]{1,0:T(4,128)} %qp_hbm.1, s32[6,400]{1,0:T(8,128)} %lat_hbm.1), custom_call_target="tpu_custom_call" | custom-call | tf_op jit(solution)/shard_map/couple/pallas_call | solution.py:544
  48.4 2.2 %reshape.3 = bf16[1,1,196608]{2,1,0:T(2,128)(2,1)} reshape(bf16[64,3072]{1,0:T(8,128)(2,1)} %couple.1) | data formatting | bytes 786432 | tf_op jit(solution)/shard_map/reshape | solution.py:606

commit v9 on v8

--- a/solution.py
+++ b/solution.py
@@ -20,7 +20,7 @@
 def kernel(
     c_hbm, vec_hbm, part_hbm, kp_hbm, qp_hbm, lat_hbm, out_ref,
     c_ref, vec_ref, part_ref, kp_ref, qp_ref, lat_ref, turned, asend, arecv, csend, crecv, cols, acols, points, grid, lat, vecs, lines, eig, part,
-    ck, sk, cq, sq, phase, wmat, wfold, bsend, brecv, table, parts, tmat, qsend, qrecv, spread,
+    ck, sk, cq, sq, phase, wmat, wfold, bsend, brecv, table, parts, far, tmat, qsend, qrecv, spread,
     a_ss, a_rs, c_ss, c_rs, b_ss, b_rs, q_ss, q_rs, z_ss, z_rs, x_ss, x_rs, m_ss, m_rs, p_ss, p_rs, in_sem, c_sem, inside,
 ):
     pb = lax.axis_index("pb")
@@ -138,9 +138,13 @@
         )
 
     def b_copy(v, h, step, other):
-        return pltpu.make_async_remote_copy(
-            src_ref=bsend.at[v, h, step], dst_ref=brecv.at[v, h, ka],
-            send_sem=b_ss.at[v, h], recv_sem=b_rs.at[v, h],
+        def piece(ref, row):
+            return ref.at[v, row] if h is None else ref.at[v, row, h]
+
+        sem = 0 if h is None else h
+        return pltpu.make_async_remote_copy(
+            src_ref=piece(bsend, step), dst_ref=piece(brecv, ka),
+            send_sem=b_ss.at[v, sem], recv_sem=b_rs.at[v, sem],
             device_id=(pb, other), device_id_type=MESH,
         )
 
@@ -154,6 +158,10 @@
     def wait_all(ref, count, sem):
         part = ref.at[pl.ds(0, count)]
         pltpu.make_async_copy(part, part, sem).wait()
+
+    def wait_pieces(ref, v, h, sems):
+        part = ref.at[v, pl.ds(0, NKA - 1), h]
+        pltpu.make_async_copy(part, part, sems.at[v, h]).wait()
 
     def loop(first, last, do):
         def step_of(step, carry):
@@ -184,7 +192,7 @@
                 [c_ref[:, :, pl.ds(first, 128)].reshape(64, 128), c_ref[:, :, pl.ds(second, 128)].reshape(64, 128)],
                 axis=0,
             )
-            turned[pl.ds(first, 128), :] = flip(both)
+            turned[pl.ds(first, 128), :] = flip(both) if t % 3 else both.T.astype(F32)
 
     def mode_of(to, v):
         field = turned[pl.ds(3 * to + v, 64, stride=48), :].astype(BF16)
@@ -263,21 +271,21 @@
         else:
             grid[...] = jnp.concatenate([across[0:NPB], jnp.zeros((NPB, 120), F32)], axis=1)
             across = jnp.concatenate([grid[pl.ds(q, 2), :] for q in order], axis=0)
-        t = jnp.zeros((across.shape[0], 2048), F32)
+        t = jnp.zeros((across.shape[0], 1536), F32)
         for axis in range(3):
             t = t + across[:, axis : axis + 1] * spots[first + axis : first + axis + 1, :]
         return t
 
     with jax.named_scope("tables"):
-        lane = lax.broadcasted_iota(jnp.int32, (1, 2048), 1)
-        inner = lax.bitwise_and(lane, 511)
+        lane = lax.broadcasted_iota(jnp.int32, (1, 1536), 1)
+        inner = lane - 1024
         folded = inner - lax.shift_right_logical(inner * 2521, 16)
         pair = jnp.where(lane < 1024, lax.shift_right_logical(lane, 1), folded)
-        second = jnp.where(lane < 1024, lax.bitwise_and(lane, 1), lax.shift_right_logical(lane - 1024, 9))
+        second = jnp.where(lane < 1024, lax.bitwise_and(lane, 1), 0)
         quarter = jnp.where(second == 1, 0.25, 0.0)
         lat[...] = jnp.zeros_like(lat)
         lat[0:6, 0:400] = lat_ref[...].astype(F32)
-        chosen = (lax.broadcasted_iota(jnp.int32, (512, 2048), 0) == pair).astype(BF16)
+        chosen = (lax.broadcasted_iota(jnp.int32, (512, 1536), 0) == pair).astype(BF16)
         spots = jnp.dot(lat[...].astype(BF16), chosen, preferred_element_type=F32)
         ang = turn(kp_ref, 0, None)
         ang = (2.0 * math.pi) * (ang - jnp.round(ang))
@@ -318,8 +326,10 @@
         s = sk[pl.ds(k, 1), :]
         for h in range(2):
             cos_q, sin_q = cq[8 * h : 8 * h + 8, :], sq[8 * h : 8 * h + 8, :]
-            both = jnp.concatenate([c * cos_q - s * sin_q, s * cos_q + c * sin_q], axis=0)
-            phase[h, step] = both.astype(BF16)
+            cosine, sine = c * cos_q - s * sin_q, s * cos_q + c * sin_q
+            phase[h, step, :, 0:1536] = jnp.concatenate([cosine, sine], axis=0).astype(BF16)
+            cosine, sine = -sine[:, 1024:1536], cosine[:, 1024:1536]
+            phase[h, step, :, 1536:2048] = jnp.concatenate([cosine, sine], axis=0).astype(BF16)
 
     with jax.named_scope("phases"):
         planes_each(make_phase)
@@ -359,34 +369,44 @@
                 imag = across(first[:, :, 1]) + second[:, :, 1]
                 both = jnp.where(low_lane, real, imag)
                 both = jnp.concatenate([both[0], both[1]], axis=1)
-                bsend[0, i2, rows] = both.astype(BF16)
+                bsend[0, rows, i2] = both.astype(BF16)
             with jax.named_scope("bloch_send"):
                 planes_each(lambda *peer: b_send(0, i2, *peer), 2 * n, 2 * n + 2)
 
         loop(0, 4, part)
-        brecv[0, i2, ka] = bsend[0, i2, NX * zi + NX - 1]
+        brecv[0, ka, i2] = bsend[0, NX * zi + NX - 1, i2]
 
     low_lane = lax.broadcasted_iota(jnp.int32, (2, 8, 8, 128), 3) < 64
 
-    def bloch_of(v):
+    def bloch_of(v, whole):
         with jax.named_scope("couplings_wait"):
             wait_all(crecv.at[v - 1], NPB - 1, c_rs.at[v - 1])
             cols[0:800] = crecv[v - 1].reshape(800, 128)
 
-        for h in range(2):
+        def half(h, first):
+            rows = pl.ds(first, 16)
+            with jax.named_scope("bloch"):
+                got = jnp.dot(
+                    phase[h, rows, :, 0:1024].reshape(256, 1024), cols[...],
+                    preferred_element_type=F32,
+                )
+                bsend[v, rows, h] = got.astype(BF16).reshape(16, 16, 128)
+
+        def send(h, first):
+            with jax.named_scope("bloch_send"):
+                planes_each(lambda *peer: b_send(v, h, *peer), first // NX, first // NX + 4)
+
+        if whole:
             for first in (0, 16):
-                rows = pl.ds(first, 16)
-                with jax.named_scope("bloch"):
-                    got = jnp.dot(
-                        phase[h, rows, :, 0:1024].reshape(256, 1024), cols[...],
-                        preferred_element_type=F32,
-                    )
-                    bsend[v, h, rows] = got.astype(BF16).reshape(16, 16, 128)
-                with jax.named_scope("bloch_send"):
-                    planes_each(lambda *peer: b_send(v, h, *peer), first // NX, first // NX + 4)
-
-        brecv[v, 0, ka] = bsend[v, 0, NX * zi + NX - 1]
-        brecv[v, 1, ka] = bsend[v, 1, NX * zi + NX - 1]
+                half(0, first)
+                half(1, first)
+                send(None, first)
+        else:
+            for h in range(2):
+                for first in (0, 16):
+                    half(h, first)
+                    send(h, first)
+        brecv[v, ka] = bsend[v, NX * zi + NX - 1]
 
     def vectors_x():
         with jax.named_scope("vectors_wait_z"):
@@ -411,15 +431,19 @@
             wait_all(table, 1, m_rs)
             wait_all(parts, NPB - 1, p_rs)
 
+            def far_of(q):
+                label = jnp.max(parts[q])
+                plane = label // NX
+                found = table[lax.rem(plane, 2), lax.rem(label, NX), plane // 2]
+                far[q] = jnp.concatenate([found, found], axis=0)
+
+            for q in range(NPB):
+                far_of(q)
+
     def squares(q, line):
         field = jnp.concatenate([tmat[t, pl.ds(line, 32, stride=8), :] for t in (0, 2, 1, 3)], axis=0)
-        label = jnp.max(parts[q])
-        plane = label // NX
-        far = table[lax.rem(plane, 2), lax.rem(label, NX), plane // 2]
-        turned_field = field.T.astype(BF16)
         got = lax.dot_general(
-            turned_field, jnp.concatenate([far, far], axis=0), (((1,), (1,)), ((), ())),
-            preferred_element_type=F32,
+            field.astype(BF16).T, far[q], (((1,), (1,)), ((), ())), preferred_element_type=F32
         )
         got = got * got
         both = got[0:64] + got[64:128]
@@ -430,12 +454,16 @@
         with jax.named_scope("bloch_wait"):
             @pl.when(n == 0)
             def _():
-                wait_all(brecv.at[0, 0], NKA - 1, b_rs.at[0, 0])
-                wait_all(brecv.at[0, 1], NKA - 1, b_rs.at[0, 1])
-
-            @pl.when(n > 1)
-            def _():
-                wait_all(brecv.at[v, h], NKA - 1, b_rs.at[v, h])
+                for i2 in range(2):
+                    wait_pieces(brecv, 0, i2, b_rs)
+
+            @pl.when(n == 2)
+            def _():
+                wait_all(brecv.at[1], NKA - 1, b_rs.at[1, 0])
+
+            @pl.when(n > 3)
+            def _():
+                wait_pieces(brecv, 2, h, b_rs)
 
         def near(t, pieces, weights):
             field = jnp.concatenate([piece.reshape(128, 128) for piece in pieces], axis=1).astype(BF16)
@@ -444,11 +472,11 @@
                 tmat[t4, pl.ds(t * 128, 128), :] = got[:, t4 * 128 : (t4 + 1) * 128]
 
         def near_folded(t):
-            fields = [brecv[0, i2, pl.ds(t * 16, 16)].astype(F32) for i2 in range(2)]
+            fields = [brecv[0, pl.ds(t * 16, 16), i2].astype(F32) for i2 in range(2)]
             near(t, [jnp.where(h == 0, field[:, 0:8], field[:, 8:16]) for field in fields], wfold)
 
         def near_other(t):
-            field = brecv[v, h, pl.ds(t * 16, 16)].astype(F32)
+            field = brecv[v, pl.ds(t * 16, 16), h].astype(F32)
             near(t, [field[:, 0:8], field[:, 8:16]], wmat)
 
         with jax.named_scope("near_rotation"):
@@ -488,10 +516,10 @@
     def _():
         vectors_x()
 
-    bloch_of(1)
+    bloch_of(1, True)
     vectors_core()
 
-    bloch_of(2)
+    bloch_of(2, False)
     vectors_done()
     loop(0, 2 * VS, rotate)
 
@@ -528,14 +556,15 @@
         wait_all(parts, NPB - 1, p_ss)
 
         def drain(v):
-            wait_all(bsend.at[v, 0], NKA - 1, b_ss.at[v, 0])
-            wait_all(bsend.at[v, 1], NKA - 1, b_ss.at[v, 1])
             wait_all(qsend.at[v], NPB - 1, q_ss.at[v])
 
         loop(0, VS, drain)
         for n in range(2):
             wait_all(asend.at[n], NPB - 1, a_ss.at[n])
             wait_all(csend.at[n], NPB - 1, c_ss.at[n])
+            wait_pieces(bsend, 0, n, b_ss)
+            wait_pieces(bsend, 2, n, b_ss)
+        wait_all(bsend.at[1], NKA - 1, b_ss.at[1, 0])
 
 
 def couple(coupling, vectors, part, kp, qp, lat):
@@ -567,17 +596,18 @@
             pltpu.VMEM((64, 128), F32),
             pltpu.VMEM((64, 128), BF16),
             pltpu.VMEM((8, 128), jnp.int32),
-            pltpu.VMEM((NKA, 2048), F32),
-            pltpu.VMEM((NKA, 2048), F32),
-            pltpu.VMEM((NPB, 2048), F32),
-            pltpu.VMEM((NPB, 2048), F32),
+            pltpu.VMEM((NKA, 1536), F32),
+            pltpu.VMEM((NKA, 1536), F32),
+            pltpu.VMEM((NPB, 1536), F32),
+            pltpu.VMEM((NPB, 1536), F32),
             pltpu.VMEM((2, NKA, 16, 2048), BF16),
             pltpu.VMEM((256, 512), BF16),
             pltpu.VMEM((256, 512), BF16),
-            pltpu.VMEM((VS, 2, NKA, 16, 128), BF16),
-            pltpu.VMEM((VS, 2, NKA, 16, 128), BF16),
+            pltpu.VMEM((VS, NKA, 2, 16, 128), BF16),
+            pltpu.VMEM((VS, NKA, 2, 16, 128), BF16),
             pltpu.VMEM((2, NX, NZ // 2, 64, 128), BF16),
             pltpu.VMEM((NPB, 8, 128), jnp.int32),
+            pltpu.VMEM((NPB, 128, 128), BF16),
             pltpu.VMEM((4, 256, 128), F32),
             pltpu.VMEM((VS, NPB, 32, 128), BF16),
             pltpu.VMEM((VS, NPB, 32, 128), BF16),

time: 50.7 us -> 50.6 us (level)
  no operation moved by 1% of the time
where the time goes in v9:
time: 50.6 us; the launch traced here: 50.5 us
  Pallas kernels  47.6 us (94%)
  local copies, waits for them, and re-layouts  2.16 us (4%)
  between operations  0.66 us (1%)
    pallas_call x1, Pallas kernels, couple(): pl.pallas_call(kernel, out_shape=jax.ShapeDtypeStruct((64, 3072), BF16),...  47.6 us
    reshape x1, local copies, waits for them, and re-layouts, body(): return out.reshape(1, 1, 196608)  2.16 us

profile of v9, /device:TPU:1, one launch (start us, length us, event | category | flops | bytes accessed | tf_op | source)
XLA Modules:
  0.0 50.5 jit_solution(5375982531624254918)
XLA Ops:
  0.7 47.6 %couple.1 = bf16[64,3072]{1,0:T(8,128)(2,1)} custom-call(bf16[25,2,6144]{2,1,0:T(2,128)(2,1)} %c_hbm.1, bf16[1,8192]{1,0:T(2,128)(2,1)} %vec_hbm.1, s32[1,1]{1,0:T(1,128)S(6)} %copy.7.part_hbm, f32[3,32]{1,0:T(4,128)} %kp_hbm.1, f32[3,16]{1,0:T(4,128)} %qp_hbm.1, s32[6,400]{1,0:T(8,128)} %lat_hbm.1), custom_call_target="tpu_custom_call" | custom-call | tf_op jit(solution)/shard_map/couple/pallas_call | solution.py:573
  48.3 2.2 %reshape.3 = bf16[1,1,196608]{2,1,0:T(2,128)(2,1)} reshape(bf16[64,3072]{1,0:T(8,128)(2,1)} %couple.1) | data formatting | bytes 786432 | tf_op jit(solution)/shard_map/reshape | solution.py:636

commit v10 on v9

--- a/solution.py
+++ b/solution.py
@@ -18,8 +18,8 @@
 
 
 def kernel(
-    c_hbm, vec_hbm, part_hbm, kp_hbm, qp_hbm, lat_hbm, out_ref,
-    c_ref, vec_ref, part_ref, kp_ref, qp_ref, lat_ref, turned, asend, arecv, csend, crecv, cols, acols, points, grid, lat, vecs, lines, eig, part,
+    c_hbm, vec_hbm, part_hbm, place_hbm, out_ref,
+    c_ref, vec_ref, part_ref, place_ref, turned, asend, arecv, csend, crecv, cols, acols, points, grid, lat, vecs, lines, eig, part,
     ck, sk, cq, sq, phase, wmat, wfold, bsend, brecv, table, parts, far, tmat, qsend, qrecv, spread,
     a_ss, a_rs, c_ss, c_rs, b_ss, b_rs, q_ss, q_rs, z_ss, z_rs, x_ss, x_rs, m_ss, m_rs, p_ss, p_rs, in_sem, c_sem, inside,
 ):
@@ -64,9 +64,7 @@
     inputs = [
         pltpu.make_async_copy(vec_hbm, vec_ref, in_sem.at[0]),
         pltpu.make_async_copy(part_hbm, part_ref, in_sem.at[1]),
-        pltpu.make_async_copy(kp_hbm, kp_ref, in_sem.at[2]),
-        pltpu.make_async_copy(qp_hbm, qp_ref, in_sem.at[3]),
-        pltpu.make_async_copy(lat_hbm, lat_ref, in_sem.at[4]),
+        pltpu.make_async_copy(place_hbm, place_ref, in_sem.at[2]),
     ]
     for copy in inputs:
         copy.start()
@@ -264,7 +262,7 @@
 
     def turn(where, first, order):
         points[...] = jnp.zeros_like(points)
-        points[0:3, 0 : where.shape[1]] = where[...]
+        points[0:3, 0 : where.shape[1]] = where
         across = points[...].T
         if order is None:
             across = across[0:NKA]
@@ -284,14 +282,14 @@
         second = jnp.where(lane < 1024, lax.bitwise_and(lane, 1), 0)
         quarter = jnp.where(second == 1, 0.25, 0.0)
         lat[...] = jnp.zeros_like(lat)
-        lat[0:6, 0:400] = lat_ref[...].astype(F32)
+        lat[0:6, 0:400] = place_ref[:, 0:400]
         chosen = (lax.broadcasted_iota(jnp.int32, (512, 1536), 0) == pair).astype(BF16)
         spots = jnp.dot(lat[...].astype(BF16), chosen, preferred_element_type=F32)
-        ang = turn(kp_ref, 0, None)
+        ang = turn(place_ref[0:3, 400:432], 0, None)
         ang = (2.0 * math.pi) * (ang - jnp.round(ang))
         ck[...] = jnp.cos(ang)
         sk[...] = jnp.sin(ang)
-        ang = turn(qp_ref, 3, [2 * lax.rem(yi + ring_offset(t, 8), 8) for t in range(8)]) + quarter
+        ang = turn(place_ref[0:3, 432:448], 3, [2 * lax.rem(yi + ring_offset(t, 8), 8) for t in range(8)]) + quarter
         ang = (2.0 * math.pi) * (ang - jnp.round(ang))
         cq[...] = jnp.cos(ang)
         sq[...] = jnp.sin(ang)
@@ -567,21 +565,19 @@
         wait_all(bsend.at[1], NKA - 1, b_ss.at[1, 0])
 
 
-def couple(coupling, vectors, part, kp, qp, lat):
+def couple(coupling, vectors, part, places):
     vmem = pl.BlockSpec(memory_space=pltpu.VMEM)
     dma = pltpu.SemaphoreType.DMA
     return pl.pallas_call(
         kernel,
         out_shape=jax.ShapeDtypeStruct((64, 3072), BF16),
-        in_specs=[pl.BlockSpec(memory_space=pltpu.HBM)] * 6,
+        in_specs=[pl.BlockSpec(memory_space=pltpu.HBM)] * 4,
         out_specs=vmem,
         scratch_shapes=[
             pltpu.VMEM((32, 2, 6144), BF16),
             pltpu.VMEM((1, 8192), BF16),
             pltpu.VMEM((1, 1), jnp.int32),
-            pltpu.VMEM((3, NKA), F32),
-            pltpu.VMEM((3, NPB), F32),
-            pltpu.VMEM((6, 400), jnp.int32),
+            pltpu.VMEM((6, 448), F32),
             pltpu.VMEM((3072, 128), F32),
             pltpu.VMEM((2, NPB, 13, 2, 128), BF16),
             pltpu.VMEM((2, NPB, 13, 2, 128), BF16),
@@ -620,19 +616,24 @@
             dma(()), dma(()),
             dma(()), dma(()),
             dma(()), dma(()),
-            dma((5,)),
+            dma((3,)),
             dma((6,)),
             pltpu.SemaphoreType.REGULAR((NZ,)),
         ],
         compiler_params=pltpu.CompilerParams(
-            collective_id=0, has_side_effects=True, vmem_limit_bytes=60 << 20
+            collective_id=0, has_side_effects=True, vmem_limit_bytes=55900000
         ),
         name="couple",
-    )(coupling, vectors, part, kp, qp, lat)
+    )(coupling, vectors, part, places)
 
 
 def body(coupling, eigvecs, partner, kpoints, qpoints, lattice):
-    out = couple(coupling, eigvecs, partner, kpoints, qpoints, lattice)
+    places = (
+        jnp.pad(lattice, ((0, 0), (0, 48))).astype(F32)
+        + jnp.pad(kpoints, ((0, 3), (400, 16)))
+        + jnp.pad(qpoints, ((0, 3), (432, 0)))
+    )
+    out = couple(coupling, eigvecs, partner, places)
     return out.reshape(1, 1, 196608)
 
 

time: 50.6 us -> 49.9 us (0.986)
  local copies, waits for them, and re-layouts: 2.16 us -> 1.17 us
  other arithmetic: 0 us -> 0.83 us
  Pallas kernels: 47.6 us -> 46.9 us
    reshape x1, local copies, waits for them, and re-layouts: 2.16 us -> 1.17 us  [body(): return out.reshape(1, 1, 196608)]
    add x0 -> x1, other arithmetic: none -> 0.83 us  [body(): jnp.pad(lattice, ((0, 0), (0, 48))).astype(F32)]
    pallas_call x1, Pallas kernels: 47.6 us -> 46.9 us  [couple(): pl.pallas_call(kernel, out_shape=jax.ShapeDtypeStruct((64, 3072), BF16),...]
where the time goes in v10:
time: 49.9 us; the launch traced here: 49.6 us
  Pallas kernels  46.9 us (94%)
  local copies, waits for them, and re-layouts  1.17 us (2%)
  other arithmetic  0.83 us (2%)
  between operations  0.67 us (1%)
    pallas_call x1, Pallas kernels, couple(): pl.pallas_call(kernel, out_shape=jax.ShapeDtypeStruct((64, 3072), BF16),...  46.9 us
    reshape x1, local copies, waits for them, and re-layouts, body(): return out.reshape(1, 1, 196608)  1.17 us

profile of v10, /device:TPU:1, one launch (start us, length us, event | category | flops | bytes accessed | tf_op | source)
XLA Modules:
  0.0 49.6 jit_solution(17068845668510983808)
XLA Ops:
  0.0 0.0 copy-start
  0.7 0.8 %pad_add_fusion.place_hbm = f32[6,448]{1,0:T(8,128)S(1)} fusion(f32[3,16]{1,0:T(4,128)} %param.10, f32[3,32]{1,0:T(4,128)} %param.9, s32[6,400]{1,0:T(8,128)} %param.11), kind=kLoop, calls=%fused_computation | loop fusion | flops 8064 | bytes 20928 | tf_op jit(solution)/shard_map/add | solution.py:632
  1.5 0.0 copy-done
  1.5 46.9 %couple.1 = bf16[64,3072]{1,0:T(8,128)(2,1)S(1)} custom-call(bf16[25,2,6144]{2,1,0:T(2,128)(2,1)} %c_hbm.1, bf16[1,8192]{1,0:T(2,128)(2,1)S(1)} %copy-done, s32[1,1]{1,0:T(1,128)S(6)} %copy.7.part_hbm, f32[6,448]{1,0:T(8,128)S(1)} %pad_add_fusion.place_hbm), custom_call_target="tpu_custom_call" | custom-call | tf_op jit(solution)/shard_map/couple/pallas_call | solution.py:571
  48.4 1.2 %reshape.3 = bf16[1,1,196608]{2,1,0:T(2,128)(2,1)} reshape(bf16[64,3072]{1,0:T(8,128)(2,1)S(1)} %couple.1) | data formatting | bytes 786432 | tf_op jit(solution)/shard_map/reshape | solution.py:637
Async XLA Ops:
  0.0 1.5 %copy-start = (bf16[1,8192]{1,0:T(2,128)(2,1)S(1)}, bf16[1,8192]{1,0:T(2,128)(2,1)}, u32[]{:S(2)}) copy-start(bf16[1,8192]{1,0:T(2,128)(2,1)} %vec_hbm.1) | copy-start | bytes 49156
